TPU v7x, 32 devices: a whole 2x2x4 slice. The times are simulated.
32 devices in a mesh: dp: 8 (over z, y), tensor: 4 (over x, core).
Axes of the slice: x: 2, y: 2, z: 4, core: 2. Of those that a mesh axis runs over, the one named last changes fastest.
Arguments:
- queries: bfloat16 [64, 6, 8192], P('dp', None, 'tensor'), may hold values from -150 to 150
- new_keys: bfloat16 [64, 6, 1024], P('dp', None, 'tensor'), may hold values from -6 to 6
- new_values: bfloat16 [64, 6, 1024], P('dp', None, 'tensor'), may hold values from -6 to 6
- key_cache: bfloat16 [64, 256, 1024], P('dp', None, 'tensor'), may hold values from -6 to 6
- value_cache: bfloat16 [64, 256, 1024], P('dp', None, 'tensor'), may hold values from -6 to 6
- cache_lengths: int32 [64], P('dp'), may hold values from 32 to 256, as said below
- accepted: int32 [64], P('tensor'), may hold values from 1 to 6
- residual: bfloat16 [64, 6, 8192], P('tensor', None, 'dp'), may hold values from -6 to 6
- out_weight: bfloat16 [8192, 8192], P('tensor', 'dp'), may hold values from -0.0625 to 0.0625
- draft_weight: bfloat16 [8192, 8192], P('tensor', 'dp'), may hold values from -0.0625 to 0.0625
Outputs:
- verified: bfloat16 [64, 6, 8192], P('tensor', None, 'dp')
- drafted: bfloat16 [5, 64, 8192], P(None, 'tensor', 'dp')
Inputs may be any that keep to these rules, and one draw needn't show every extreme that they name: `cache_lengths`: every draw has a window with all 256 slots live.
All inputs are finite; a program needn't handle non-finite values.
Results may differ from a plain program's by a relative error of at most 0.008.
Values may be sent and summed in bfloat16 or wider, within the bound.
A program may use at most 64 MiB of HBM per device.

v0:
```python
import jax
import jax.numpy as jnp
from jax import lax
from jax.sharding import PartitionSpec as P

HD = 128
STEPS = 5


def widen(drafted_rows):
    wide_rows = lax.all_gather(drafted_rows, "dp", axis=1, tiled=True)
    return lax.all_to_all(wide_rows, "tensor", split_axis=1, concat_axis=0, tiled=True)


def per_device(
    queries,
    new_keys,
    new_values,
    key_cache,
    value_cache,
    cache_lengths,
    accepted,
    residual,
    out_weight,
    draft_weight,
):
    windows_here, tokens_here, query_width = queries.shape
    cache_size = key_cache.shape[1]
    kv_here = new_keys.shape[2] // HD
    group_size = query_width // HD // kv_here
    query_split = queries.reshape(windows_here, tokens_here, kv_here, group_size, HD)
    keys_cached = key_cache.reshape(windows_here, cache_size, kv_here, HD)
    keys_fresh = new_keys.reshape(windows_here, tokens_here, kv_here, HD)
    score_cache = jnp.einsum(
        "wtkgd,wpkd->wkgtp", query_split, keys_cached, preferred_element_type=jnp.float32
    ) * HD ** (-0.5)
    score_fresh = jnp.einsum(
        "wtkgd,wpkd->wkgtp", query_split, keys_fresh, preferred_element_type=jnp.float32
    ) * HD ** (-0.5)
    live_cache = (jnp.arange(cache_size)[None, :] < cache_lengths[:, None])[:, None, None, None, :]
    live_fresh = jnp.arange(tokens_here)[None, :] <= jnp.arange(tokens_here)[:, None]
    scores = jnp.concatenate(
        [
            jnp.where(live_cache, score_cache, -jnp.inf),
            jnp.where(live_fresh, score_fresh, -jnp.inf),
        ],
        axis=-1,
    )
    largest = jnp.max(scores, axis=-1, keepdims=True)
    powered = jnp.exp(scores - largest)
    weights = (powered / jnp.sum(powered, axis=-1, keepdims=True)).astype(jnp.bfloat16)
    values_cached = value_cache.reshape(windows_here, cache_size, kv_here, HD)
    values_fresh = new_values.reshape(windows_here, tokens_here, kv_here, HD)
    mixed_rows = jnp.einsum(
        "wkgtp,wpkd->wtkgd",
        weights[..., :cache_size],
        values_cached,
        preferred_element_type=jnp.float32,
    )
    mixed_rows = mixed_rows + jnp.einsum(
        "wkgtp,wpkd->wtkgd",
        weights[..., cache_size:],
        values_fresh,
        preferred_element_type=jnp.float32,
    )
    attended = mixed_rows.astype(jnp.bfloat16).reshape(windows_here * tokens_here, query_width)
    partial_out = jnp.dot(
        lax.all_gather(attended, "dp", axis=0, tiled=True),
        out_weight,
        preferred_element_type=jnp.float32,
    )
    summed = lax.psum_scatter(partial_out, "tensor", scatter_dimension=0, tiled=True)
    block_windows, block_tokens, block_cols = residual.shape
    flat_residual = residual.reshape(block_windows * block_tokens, block_cols).astype(jnp.float32)
    verified = (
        (flat_residual + summed)
        .astype(jnp.bfloat16)
        .reshape(block_windows, block_tokens, block_cols)
    )
    chosen = jnp.arange(block_tokens)[None, :] == (accepted - 1)[:, None]
    picked = jnp.sum(
        jnp.where(chosen[:, :, None], verified, jnp.zeros((), jnp.bfloat16)),
        axis=1,
        dtype=jnp.bfloat16,
    )
    results = []
    current = widen(picked)
    row_block = current.shape[0] // lax.axis_size("tensor")
    row_start = lax.axis_index("tensor") * row_block
    for draft_step in range(STEPS):
        everyone = lax.psum(
            jnp.dot(current, draft_weight, preferred_element_type=jnp.float32), "tensor"
        )
        share = lax.dynamic_slice_in_dim(everyone, row_start, row_block, 0)
        drafted_now = jnp.tanh(2.0 * share).astype(jnp.bfloat16)
        results.append(drafted_now)
        if draft_step + 1 < STEPS:
            current = widen(drafted_now)
    return (verified, jnp.stack(results))


def solution(mesh):
    placed = (
        P("dp", None, "tensor"),
        P("dp", None, "tensor"),
        P("dp", None, "tensor"),
        P("dp", None, "tensor"),
        P("dp", None, "tensor"),
        P("dp"),
        P("tensor"),
        P("tensor", None, "dp"),
        P("tensor", "dp"),
        P("tensor", "dp"),
    )
    return jax.shard_map(
        per_device,
        mesh=mesh,
        in_specs=placed,
        out_specs=(P("tensor", None, "dp"), P(None, "tensor", "dp")),
        check_vma=False,
    )
```

profile of v0, /device:TPU:0, one launch (start us, length us, event | category | flops | bytes accessed | tf_op | source)
XLA Modules:
  0.0 483.4 jit_solution(9982029606492289622)
XLA Ops:
  7.2 1.4 reshape.87
  8.6 0.8 iota_compare_fusion.1
  9.4 1.7 fusion.11
  11.1 0.2 fusion.18
  11.4 0.6 copy.104
  12.0 0.5 fusion.19
  12.6 0.4 fusion.8
  13.0 0.3 divide_convert_fusion
  13.4 0.3 reshape.90
  13.6 0.3 fusion.5
  13.9 0.2 fusion.4
  14.2 0.8 reshape.92
  15.0 47.0 %all-gather.2.cloned.1.call-done = bf16[384,2048]{1,0:T(8,128)(2,1)} async-done(((bf16[48,2048]{1,0:T(8,128)(2,1)}), bf16[384,2048]{1,0:T(8,128)(2,1)}) %all-gather.2.cloned.1.call-update) | async-done | bytes 1572880 | tf_op jit(solution)/shard_map/all_gather | solution.py:68
  62.0 5.6 %fusion.20 = f32[384,1024]{1,0:T(8,128)} fusion(bf16[384,2048]{1,0:T(8,128)(2,1)} %all-gather.2.cloned.1.call-done, bf16[2048,1024]{1,0:T(8,128)(2,1)} %param.18), kind=kOutput, calls=%fused_computation.47 | convolution fusion | flops 1610612736 | bytes 7340032 | tf_op jit(solution)/shard_map/dot_general | solution.py:67
  67.7 0.1 copy.98
  67.8 0.1 reshape.94
  67.9 0.1 iota_compare_fusion
  68.0 26.8 %reduce-scatter.2.cloned.1.call-done = f32[96,1024]{1,0:T(8,128)} async-done(((f32[384,1024]{1,0:T(8,128)}), f32[96,1024]{1,0:T(8,128)}) %reduce-scatter.2.cloned.1.call-update) | async-done | bytes 393232 | tf_op jit(solution)/shard_map/reduce_scatter | solution.py:72
  94.8 1.0 add_convert_fusion
  95.8 0.1 reshape.93
  95.9 0.2 select_reduce_fusion
  96.1 30.8 %all_gather.19 = bf16[16,8192]{1,0:T(8,128)(2,1)S(1)} all-gather(bf16[16,1024]{1,0:T(8,128)(2,1)S(1)} %select_reduce_fusion), channel_id=1, replica_groups=mesh['dp'=8,'tensor'=4] {'dp'}, dimensions={1}, use_global_device_ids=true | all-gather | bytes 294912 | tf_op jit(solution)/shard_map/all_gather | solution.py:11
  126.9 8.4 %all_to_all.95 = bf16[16,4,2048]{2,0,1:T(8,128)(2,1)S(1)} all-to-all(bf16[16,4,2048]{2,0,1:T(8,128)(2,1)S(1)} %bitcast.87), channel_id=1, replica_groups=mesh['dp'=8,'tensor'=4] {'tensor'}, dimensions={1} | all-to-all | bytes 524288 | tf_op jit(solution)/shard_map/all_to_all | solution.py:12
  135.4 3.7 fusion.21
  139.2 32.0 %all-reduce.6.cloned.1.call-done = f32[64,1024]{1,0:T(8,128)} async-done(((f32[64,1024]{1,0:T(8,128)}), f32[64,1024]{1,0:T(8,128)}) %all-reduce.6.cloned.1.call-update) | async-done | bytes 262160 | tf_op jit(solution)/shard_map/psum | solution.py:91
  171.2 0.9 bitcast_dynamic-update-slice_fusion.3
  172.1 31.0 %all_gather.20 = bf16[16,8192]{1,0:T(8,128)(2,1)S(1)} all-gather(bf16[16,1024]{1,0:T(8,128)(2,1)S(1)} %get-tuple-element.23), channel_id=1, replica_groups=mesh['dp'=8,'tensor'=4] {'dp'}, dimensions={1}, use_global_device_ids=true | all-gather | bytes 294912 | tf_op jit(solution)/shard_map/all_gather | solution.py:11
  203.0 8.4 %all_to_all.96 = bf16[16,4,2048]{2,0,1:T(8,128)(2,1)S(1)} all-to-all(bf16[16,4,2048]{2,0,1:T(8,128)(2,1)S(1)} %bitcast.89), channel_id=1, replica_groups=mesh['dp'=8,'tensor'=4] {'tensor'}, dimensions={1} | all-to-all | bytes 524288 | tf_op jit(solution)/shard_map/all_to_all | solution.py:12
  211.5 3.7 fusion.22
  215.3 31.9 %all-reduce.8.cloned.1.call-done = f32[64,1024]{1,0:T(8,128)} async-done(((f32[64,1024]{1,0:T(8,128)}), f32[64,1024]{1,0:T(8,128)}) %all-reduce.8.cloned.1.call-update) | async-done | bytes 262160 | tf_op jit(solution)/shard_map/psum | solution.py:91
  247.1 0.9 bitcast_dynamic-update-slice_fusion.2
  248.0 31.0 %all_gather.21 = bf16[16,8192]{1,0:T(8,128)(2,1)S(1)} all-gather(bf16[16,1024]{1,0:T(8,128)(2,1)S(1)} %get-tuple-element.21), channel_id=1, replica_groups=mesh['dp'=8,'tensor'=4] {'dp'}, dimensions={1}, use_global_device_ids=true | all-gather | bytes 294912 | tf_op jit(solution)/shard_map/all_gather | solution.py:11
  279.0 8.4 %all_to_all.97 = bf16[16,4,2048]{2,0,1:T(8,128)(2,1)S(1)} all-to-all(bf16[16,4,2048]{2,0,1:T(8,128)(2,1)S(1)} %bitcast.91), channel_id=1, replica_groups=mesh['dp'=8,'tensor'=4] {'tensor'}, dimensions={1} | all-to-all | bytes 524288 | tf_op jit(solution)/shard_map/all_to_all | solution.py:12
  287.4 3.7 fusion.23
  291.2 31.9 %all-reduce.10.cloned.1.call-done = f32[64,1024]{1,0:T(8,128)} async-done(((f32[64,1024]{1,0:T(8,128)}), f32[64,1024]{1,0:T(8,128)}) %all-reduce.10.cloned.1.call-update) | async-done | bytes 262160 | tf_op jit(solution)/shard_map/psum | solution.py:91
  323.1 0.9 bitcast_dynamic-update-slice_fusion.1
  323.9 31.0 %all_gather.22 = bf16[16,8192]{1,0:T(8,128)(2,1)S(1)} all-gather(bf16[16,1024]{1,0:T(8,128)(2,1)S(1)} %get-tuple-element.19), channel_id=1, replica_groups=mesh['dp'=8,'tensor'=4] {'dp'}, dimensions={1}, use_global_device_ids=true | all-gather | bytes 294912 | tf_op jit(solution)/shard_map/all_gather | solution.py:11
  354.9 8.4 %all_to_all.98 = bf16[16,4,2048]{2,0,1:T(8,128)(2,1)S(1)} all-to-all(bf16[16,4,2048]{2,0,1:T(8,128)(2,1)S(1)} %bitcast.93), channel_id=1, replica_groups=mesh['dp'=8,'tensor'=4] {'tensor'}, dimensions={1} | all-to-all | bytes 524288 | tf_op jit(solution)/shard_map/all_to_all | solution.py:12
  363.4 3.7 fusion.24
  367.2 31.9 %all-reduce.12.cloned.1.call-done = f32[64,1024]{1,0:T(8,128)} async-done(((f32[64,1024]{1,0:T(8,128)}), f32[64,1024]{1,0:T(8,128)}) %all-reduce.12.cloned.1.call-update) | async-done | bytes 262160 | tf_op jit(solution)/shard_map/psum | solution.py:91
  399.0 0.9 bitcast_dynamic-update-slice_fusion
  399.9 31.0 %all_gather.23 = bf16[16,8192]{1,0:T(8,128)(2,1)S(1)} all-gather(bf16[16,1024]{1,0:T(8,128)(2,1)S(1)} %get-tuple-element.17), channel_id=1, replica_groups=mesh['dp'=8,'tensor'=4] {'dp'}, dimensions={1}, use_global_device_ids=true | all-gather | bytes 294912 | tf_op jit(solution)/shard_map/all_gather | solution.py:11
  430.9 8.4 %all_to_all.99 = bf16[16,4,2048]{2,0,1:T(8,128)(2,1)S(1)} all-to-all(bf16[16,4,2048]{2,0,1:T(8,128)(2,1)S(1)} %bitcast.95), channel_id=1, replica_groups=mesh['dp'=8,'tensor'=4] {'tensor'}, dimensions={1} | all-to-all | bytes 524288 | tf_op jit(solution)/shard_map/all_to_all | solution.py:12
  439.3 3.7 fusion.25
  443.1 0.8 copy.114
  443.9 31.1 %all-reduce.14.cloned.1.call-done = f32[64,1024]{1,0:T(8,128)} async-done(((f32[64,1024]{1,0:T(8,128)}), f32[64,1024]{1,0:T(8,128)}) %all-reduce.14.cloned.1.call-update) | async-done | bytes 262160 | tf_op jit(solution)/shard_map/psum | solution.py:91
  475.0 0.9 fusion.15
  475.9 0.7 copy-done.4
  (34 shorter events, 0.6 us)
Async XLA Ops:
  7.2 2.3 copy-start
  7.2 54.8 %all-gather.2.cloned.1.call-start = ((), (), s32[]{:S(2)}) async-start(), calls=%async_computation.6 | async-start | bytes 1769472 | tf_op jit(solution)/shard_map/all_gather | solution.py:68
  8.6 4.7 copy-start.1
  12.6 1.4 copy-start.3
  15.0 52.7 %copy-start.2 = (bf16[16,6,1024]{2,0,1:T(8,128)(2,1)S(1)}, bf16[16,6,1024]{2,0,1:T(8,128)(2,1)}, u32[]{:S(2)}) copy-start(bf16[16,6,1024]{2,0,1:T(8,128)(2,1)} %param.17) | copy-start | bytes 589828
  15.0 52.9 %copy-start.5 = (s32[16]{0:T(128)S(1)}, s32[16]{0:T(128)}, u32[]{:S(2)}) copy-start(s32[16]{0:T(128)} %param.16) | copy-start | bytes 196
  15.0 79.8 %reduce-scatter.2.cloned.1.call-start = ((), (), s32[]{:S(2)}) async-start(), calls=%async_computation.7 | async-start | bytes 1966080 | tf_op jit(solution)/shard_map/reduce_scatter | solution.py:72
  67.7 103.5 %all-reduce.6.cloned.1.call-start = ((), (), s32[]{:S(2)}) async-start(), calls=%async_computation.8 | async-start | bytes 524288 | tf_op jit(solution)/shard_map/psum | solution.py:91
  139.1 108.0 %all-reduce.8.cloned.1.call-start = ((), (), s32[]{:S(2)}) async-start(), calls=%async_computation.9 | async-start | bytes 524288 | tf_op jit(solution)/shard_map/psum | solution.py:91
  215.2 107.9 %all-reduce.10.cloned.1.call-start = ((), (), s32[]{:S(2)}) async-start(), calls=%async_computation.10 | async-start | bytes 524288 | tf_op jit(solution)/shard_map/psum | solution.py:91
  291.2 107.9 %all-reduce.12.cloned.1.call-start = ((), (), s32[]{:S(2)}) async-start(), calls=%async_computation.11 | async-start | bytes 524288 | tf_op jit(solution)/shard_map/psum | solution.py:91
  367.1 107.9 %all-reduce.14.cloned.1.call-start = ((), (), s32[]{:S(2)}) async-start(), calls=%async_computation.12 | async-start | bytes 524288 | tf_op jit(solution)/shard_map/psum | solution.py:91
  475.8 0.7 copy-start.4
Sparse Core Ops, SparseCore 0:
  15.1 46.8 all-gather.1
  67.8 26.9 reduce-scatter.1
  139.2 31.9 all-reduce.5
  215.3 31.7 all-reduce.7
  291.3 31.7 all-reduce.9
  367.2 31.7 all-reduce.11
  443.2 31.7 all-reduce.13
where the time goes:
time: 484 us; the launch traced here: 483 us
  waiting for transfers between devices  233 us (48%)
  blocking collectives  197 us (41%)
  matrix products  26.9 us (6%)
  between operations  14.4 us (3%)
  other arithmetic  7.38 us (2%)
  local copies, waits for them, and re-layouts  4.92 us (1%)
    psum x5, waiting for transfers between devices, per_device(): lax.psum(jnp.dot(current, draft_weight, preferred_element_type=jnp.float3...  159 us
    all_gather x5, blocking collectives, widen(): wide_rows = lax.all_gather(drafted_rows, 'dp', axis=1, tiled=True)  155 us
    all_gather x1, waiting for transfers between devices, per_device(): lax.all_gather(attended, 'dp', axis=0, tiled=True)  47 us
    all_to_all x5, blocking collectives, widen(): lax.all_to_all(wide_rows, 'tensor', split_axis=1, concat_axis=0, tiled=True)  42.1 us
    reduce_scatter x1, waiting for transfers between devices, per_device(): lax.psum_scatter(partial_out, 'tensor', scatter_dimension=0, tiled=True)  26.8 us
    dot_general x5, matrix products, per_device(): jnp.dot(current, draft_weight, preferred_element_type=jnp.float32)  18.6 us
  transfers between devices with their start and end apart: 7, of which 7 were waited for; matrix products, arithmetic and copies ran while one was open for 0% of the time, Pallas kernels for 0%

commit v1 on v0

--- a/solution.py
+++ b/solution.py
@@ -1,15 +1,206 @@
+import functools
+
 import jax
 import jax.numpy as jnp
 from jax import lax
+from jax.experimental import pallas as pl
+from jax.experimental.pallas import tpu as pltpu
 from jax.sharding import PartitionSpec as P
 
 HD = 128
 STEPS = 5
 
 
-def widen(drafted_rows):
-    wide_rows = lax.all_gather(drafted_rows, "dp", axis=1, tiled=True)
-    return lax.all_to_all(wide_rows, "tensor", split_axis=1, concat_axis=0, tiled=True)
+MESH = pl.DeviceIdType.MESH
+BF16 = jnp.bfloat16
+F32 = jnp.float32
+
+
+def draft_kernel(
+    nt,
+    nd,
+    picked_ref,
+    weight_hbm,
+    out_ref,
+    weight,
+    pieces,
+    spread,
+    feats,
+    partial,
+    outgoing,
+    landed,
+    weight_sem,
+    spread_send,
+    spread_recv,
+    feat_send,
+    feat_recv,
+    part_send,
+    part_recv,
+):
+    rows, cols = picked_ref.shape
+    minors = nd // nt
+    me_t = lax.axis_index("tensor")
+    me_d = lax.axis_index("dp")
+    group = me_d // minors
+    minor = me_d % minors
+
+    load = pltpu.make_async_copy(weight_hbm, weight, weight_sem)
+    load.start()
+    barrier = pltpu.get_barrier_semaphore()
+    for k in range(nt):
+        for j in range(minors):
+            if k or j:
+                peer = (group * minors + (minor + j) % minors, (me_t + k) % nt)
+                pl.semaphore_signal(barrier, inc=1, device_id=peer, device_id_type=MESH)
+    for i in range(1, nt):
+        peer = ((group + i) % nt * minors + minor, me_t)
+        pl.semaphore_signal(barrier, inc=1, device_id=peer, device_id_type=MESH)
+    pieces[0] = picked_ref[...]
+    pl.semaphore_wait(barrier, nt * minors - 1 + nt - 1)
+    load.wait()
+
+    def spread_copy(s, i):
+        return pltpu.make_async_remote_copy(
+            src_ref=pieces.at[s],
+            dst_ref=spread.at[s, i - 1],
+            send_sem=spread_send.at[s, i - 1],
+            recv_sem=spread_recv.at[s, i - 1],
+            device_id=((group + i) % nt * minors + minor, me_t),
+            device_id_type=MESH,
+        )
+
+    def feat_slot(s):
+        return feats.at[
+            s,
+            pl.ds(pl.multiple_of(me_t * rows, rows), rows),
+            pl.ds(pl.multiple_of(minor * cols, cols), cols),
+        ]
+
+    def feat_copy(s, i, j):
+        return pltpu.make_async_remote_copy(
+            src_ref=pieces.at[s] if i == 0 else spread.at[s, i - 1],
+            dst_ref=feat_slot(s),
+            send_sem=feat_send.at[s, i, j],
+            recv_sem=feat_recv.at[s, me_t, minor],
+            device_id=(group * minors + (minor + j) % minors, (group + nt - i) % nt),
+            device_id_type=MESH,
+        )
+
+    def feat_local(s, i):
+        return pltpu.make_async_copy(
+            pieces.at[s] if i == 0 else spread.at[s, i - 1],
+            feat_slot(s),
+            feat_recv.at[s, me_t, minor],
+        )
+
+    def part_copy(s, k):
+        return pltpu.make_async_remote_copy(
+            src_ref=outgoing.at[s, pl.ds(pl.multiple_of((me_t + k) % nt * rows, rows), rows)],
+            dst_ref=landed.at[s, k - 1],
+            send_sem=part_send.at[s, k - 1],
+            recv_sem=part_recv.at[s, k - 1],
+            device_id=(me_d, (me_t + k) % nt),
+            device_id_type=MESH,
+        )
+
+    order = sorted(range(nt), key=lambda i: min(i, nt - i))
+
+    def step(s, carry):
+        for i in order[1:]:
+            spread_copy(s, i).start()
+        for i in order:
+            if i:
+                spread_copy(s, i).wait_recv()
+            target = (group + nt - i) % nt
+            for j in range(1, minors):
+                feat_copy(s, i, j).start()
+
+            @pl.when(target != me_t)
+            def _():
+                feat_copy(s, i, 0).start()
+
+            @pl.when(target == me_t)
+            def _():
+                feat_local(s, i).start()
+
+        for t in range(nt):
+            for m in range(minors):
+                pltpu.make_async_copy(
+                    pieces.at[s],
+                    feats.at[s, pl.ds(t * rows, rows), pl.ds(m * cols, cols)],
+                    feat_recv.at[s, t, m],
+                ).wait()
+        for c in range(0, cols, 256):
+            product = jnp.dot(
+                feats[s], weight[:, c : c + 256], preferred_element_type=F32
+            )
+            partial[:, c : c + 256] = product
+            outgoing[s, :, c : c + 256] = product.astype(BF16)
+        for k in range(1, nt):
+            part_copy(s, k).start()
+        total = partial[pl.ds(pl.multiple_of(me_t * rows, rows), rows), :]
+        for k in range(1, nt):
+            part_copy(s, k).wait_recv()
+            total = total + landed[s, k - 1].astype(F32)
+        drafted = jnp.tanh(2.0 * total).astype(BF16)
+        out_ref[s] = drafted
+        pieces[s + 1] = drafted
+        return carry
+
+    lax.fori_loop(0, STEPS, step, 0)
+
+    def drain(s, carry):
+        for i in range(nt):
+            if i:
+                spread_copy(s, i).wait_send()
+                part_copy(s, i).wait_send()
+            for j in range(1, minors):
+                feat_copy(s, i, j).wait_send()
+
+            @pl.when((group + nt - i) % nt != me_t)
+            def _():
+                feat_copy(s, i, 0).wait_send()
+
+        return carry
+
+    lax.fori_loop(0, STEPS, drain, 0)
+
+
+def draft(nt, nd, picked, draft_weight):
+    rows, cols = picked.shape
+    depth = draft_weight.shape[0]
+    minors = nd // nt
+    dma = pltpu.SemaphoreType.DMA
+    return pl.pallas_call(
+        functools.partial(draft_kernel, nt, nd),
+        out_shape=jax.ShapeDtypeStruct((STEPS, rows, cols), BF16),
+        in_specs=[pl.BlockSpec(memory_space=pltpu.VMEM), pl.BlockSpec(memory_space=pl.ANY)],
+        out_specs=pl.BlockSpec(memory_space=pltpu.VMEM),
+        scratch_shapes=[
+            pltpu.VMEM((depth, cols), BF16),
+            pltpu.VMEM((STEPS + 1, rows, cols), BF16),
+            pltpu.VMEM((STEPS, nt - 1, rows, cols), BF16),
+            pltpu.VMEM((STEPS, nt * rows, depth), BF16),
+            pltpu.VMEM((nt * rows, cols), F32),
+            pltpu.VMEM((STEPS, nt * rows, cols), BF16),
+            pltpu.VMEM((STEPS, nt - 1, rows, cols), BF16),
+            dma,
+            dma((STEPS, nt - 1)),
+            dma((STEPS, nt - 1)),
+            dma((STEPS, nt, minors)),
+            dma((STEPS, nt, minors)),
+            dma((STEPS, nt - 1)),
+            dma((STEPS, nt - 1)),
+        ],
+        compiler_params=pltpu.CompilerParams(
+            collective_id=0, has_side_effects=True, vmem_limit_bytes=40 * 1024 * 1024
+        ),
+        cost_estimate=pl.CostEstimate(
+            flops=2 * STEPS * nt * rows * depth * cols,
+            bytes_accessed=2 * depth * cols,
+            transcendentals=STEPS * rows * cols,
+        ),
+    )(picked, draft_weight)
 
 
 def per_device(
@@ -83,20 +274,8 @@
         axis=1,
         dtype=jnp.bfloat16,
     )
-    results = []
-    current = widen(picked)
-    row_block = current.shape[0] // lax.axis_size("tensor")
-    row_start = lax.axis_index("tensor") * row_block
-    for draft_step in range(STEPS):
-        everyone = lax.psum(
-            jnp.dot(current, draft_weight, preferred_element_type=jnp.float32), "tensor"
-        )
-        share = lax.dynamic_slice_in_dim(everyone, row_start, row_block, 0)
-        drafted_now = jnp.tanh(2.0 * share).astype(jnp.bfloat16)
-        results.append(drafted_now)
-        if draft_step + 1 < STEPS:
-            current = widen(drafted_now)
-    return (verified, jnp.stack(results))
+    drafted = draft(lax.axis_size("tensor"), lax.axis_size("dp"), picked, draft_weight)
+    return (verified, drafted)
 
 
 def solution(mesh):

time: 484 us -> 170 us (0.35)
  blocking collectives: 197 us -> 0 us
  waiting for transfers between devices: 233 us -> 72.5 us
  Pallas kernels: 0 us -> 63.6 us
  matrix products: 26.9 us -> 7.59 us
  other arithmetic: 7.38 us -> 2.38 us
    psum x5 -> x0, waiting for transfers between devices: 159 us -> none  [per_device(): lax.psum(jnp.dot(current, draft_weight, preferred_element_type=jnp.float3...]
    all_gather x5 -> x0, blocking collectives: 155 us -> none  [widen(): wide_rows = lax.all_gather(drafted_rows, 'dp', axis=1, tiled=True)]
    pallas_call x0 -> x1, Pallas kernels: none -> 63.6 us  [draft(): pl.pallas_call(functools.partial(draft_kernel, nt, nd), out_shape=jax.Sha...]
    all_to_all x5 -> x0, blocking collectives: 42.1 us -> none  [widen(): lax.all_to_all(wide_rows, 'tensor', split_axis=1, concat_axis=0, tiled=True)]
    dot_general x5 -> x0, matrix products: 18.6 us -> none  [per_device(): jnp.dot(current, draft_weight, preferred_element_type=jnp.float32)]
    unnamed x13 -> x18, local copies, waits for them, and re-layouts: 1.49 us -> 6.38 us
  transfers between devices with their start and end apart: 7 -> 2, of which waited for: 7 -> 2; matrix products, arithmetic and copies ran while one was open for 0% -> 0% of each run, Pallas kernels for 0% -> 0%
where the time goes in v1:
time: 170 us
  waiting for transfers between devices  72.5 us (43%)
  Pallas kernels  63.6 us (37%)
  between operations  14.2 us (8%)
  local copies, waits for them, and re-layouts  9.71 us (6%)
  matrix products  7.59 us (4%)
  other arithmetic  2.38 us (1%)
    pallas_call x1, Pallas kernels, draft(): pl.pallas_call(functools.partial(draft_kernel, nt, nd), out_shape=jax.Sha...  63.6 us
    all_gather x1, waiting for transfers between devices, per_device(): lax.all_gather(attended, 'dp', axis=0, tiled=True)  47 us
    reduce_scatter x1, waiting for transfers between devices, per_device(): lax.psum_scatter(partial_out, 'tensor', scatter_dimension=0, tiled=True)  25.5 us
    unnamed x18, local copies, waits for them, and re-layouts  6.38 us
    dot_general x1, matrix products, per_device(): jnp.dot(lax.all_gather(attended, 'dp', axis=0, tiled=True), out_weight, p...  5.61 us
  transfers between devices with their start and end apart: 2, of which 2 were waited for; matrix products, arithmetic and copies ran while one was open for 0% of the time, Pallas kernels for 0%

profile of v1, /device:TPU:0, one launch (start us, length us, event | category | flops | bytes accessed | tf_op | source)
XLA Modules:
  0.0 170.1 jit_solution(18351465353191991753)
XLA Ops:
  7.2 0.0 copy-start
  7.2 0.0 copy-start.6
  7.2 0.0 copy-start.4
  7.2 0.0 all-gather.2.cloned.1.call-start
  7.3 1.4 reshape.72
  8.6 0.0 copy-done.6
  8.7 0.1 iota_compare_fusion.1
  8.7 0.0 copy-done
  8.7 0.0 copy-done.4
  8.7 1.0 fusion.11
  9.7 0.2 fusion.16
  9.9 0.6 copy.60
  10.6 0.6 fusion.17
  11.1 0.4 fusion.8
  11.6 0.0 copy-start.2
  11.6 0.3 divide_convert_fusion
  11.9 0.9 copy-done.2
  12.8 0.3 reshape.75
  13.1 0.0 copy-start.5
  13.1 0.3 fusion.5
  13.4 0.4 copy-done.5
  13.8 0.2 fusion.4
  14.1 0.8 reshape.77
  14.8 0.0 all-gather.2.cloned.1.call-update
  14.8 0.0 reduce-scatter.2.cloned.1.call-start
  14.9 47.0 %all-gather.2.cloned.1.call-done = bf16[384,2048]{1,0:T(8,128)(2,1)} async-done(((bf16[48,2048]{1,0:T(8,128)(2,1)}), bf16[384,2048]{1,0:T(8,128)(2,1)}) %all-gather.2.cloned.1.call-update) | async-done | bytes 1572880 | tf_op jit(solution)/shard_map/all_gather | solution.py:259
  61.9 5.6 %fusion.18 = f32[384,1024]{1,0:T(8,128)} fusion(bf16[384,2048]{1,0:T(8,128)(2,1)} %all-gather.2.cloned.1.call-done, bf16[2048,1024]{1,0:T(8,128)(2,1)} %param.18), kind=kOutput, calls=%fused_computation.31 | convolution fusion | flops 1610612736 | bytes 7340032 | tf_op jit(solution)/shard_map/dot_general | solution.py:258
  67.5 0.0 copy-start.3
  67.5 0.0 reduce-scatter.2.cloned.1.call-update
  67.5 0.9 copy-done.3
  68.4 0.0 copy-start.7
  68.4 0.1 copy.54
  68.5 0.1 reshape.79
  68.6 0.5 copy-done.7
  69.1 0.1 iota_compare_fusion
  69.2 25.5 %reduce-scatter.2.cloned.1.call-done = f32[96,1024]{1,0:T(8,128)} async-done(((f32[384,1024]{1,0:T(8,128)}), f32[96,1024]{1,0:T(8,128)}) %reduce-scatter.2.cloned.1.call-update) | async-done | bytes 393232 | tf_op jit(solution)/shard_map/reduce_scatter | solution.py:263
  94.7 1.0 add_convert_fusion
  95.7 0.1 reshape.78
  95.8 0.8 copy.65
  96.6 0.2 select_reduce_fusion.picked_ref
  96.8 0.0 copy-start.1
  96.8 2.2 %copy-done.1 = bf16[2048,1024]{1,0:T(8,128)(2,1)S(1)} copy-done((bf16[2048,1024]{1,0:T(8,128)(2,1)S(1)}, bf16[2048,1024]{1,0:T(8,128)(2,1)}, u32[]{:S(2)}) %copy-start.1) | copy-done | bytes 4194328
  99.0 63.6 %shard_map.113 = bf16[5,16,1024]{2,1,0:T(8,128)(2,1)S(1)} custom-call(bf16[16,1024]{1,0:T(8,128)(2,1)S(1)} %select_reduce_fusion.picked_ref, bf16[2048,1024]{1,0:T(8,128)(2,1)S(1)} %copy-done.1), custom_call_target="tpu_custom_call" | custom-call | flops 1342177280 | bytes 4194304 | tf_op jit(solution)/shard_map/pallas_call | solution.py:174
  162.5 0.7 copy.100
  (4 shorter events, 0.1 us)
Async XLA Ops:
  7.2 1.6 copy-start
  7.2 1.5 copy-start.6
  7.2 1.5 copy-start.4
  7.2 54.7 %all-gather.2.cloned.1.call-start = ((), (), s32[]{:S(2)}) async-start(), calls=%async_computation.1 | async-start | bytes 1769472 | tf_op jit(solution)/shard_map/all_gather | solution.py:259
  11.6 1.2 copy-start.2
  13.1 0.7 copy-start.5
  14.8 79.8 %reduce-scatter.2.cloned.1.call-start = ((), (), s32[]{:S(2)}) async-start(), calls=%async_computation.2 | async-start | bytes 1966080 | tf_op jit(solution)/shard_map/reduce_scatter | solution.py:263
  67.5 0.9 copy-start.3
  68.4 0.7 copy-start.7
  96.8 2.2 %copy-start.1 = (bf16[2048,1024]{1,0:T(8,128)(2,1)S(1)}, bf16[2048,1024]{1,0:T(8,128)(2,1)}, u32[]{:S(2)}) copy-start(bf16[2048,1024]{1,0:T(8,128)(2,1)} %weight_hbm.1) | copy-start | bytes 12582916
Sparse Core Ops, SparseCore 0:
  15.0 46.8 all-gather.1
  67.6 26.9 reduce-scatter.1

commit v2 on v1

--- a/solution.py
+++ b/solution.py
@@ -16,36 +16,64 @@
 F32 = jnp.float32
 
 
-def draft_kernel(
+def decode_kernel(
     nt,
     nd,
-    picked_ref,
-    weight_hbm,
-    out_ref,
-    weight,
+    attended_ref,
+    accepted_ref,
+    residual_ref,
+    out_weight_hbm,
+    draft_weight_hbm,
+    verified_ref,
+    drafted_ref,
+    out_weight,
+    draft_weight,
+    accepted_near,
+    first,
     pieces,
     spread,
     feats,
     partial,
     outgoing,
     landed,
+    rows_all,
+    rows_own,
+    rows_out,
+    rows_in,
     weight_sem,
+    accepted_send,
+    accepted_recv,
+    first_send,
+    first_pass,
+    first_recv,
     spread_send,
     spread_recv,
     feat_send,
     feat_recv,
     part_send,
     part_recv,
+    all_send,
+    all_pass,
+    all_recv,
+    rows_send,
+    rows_recv,
 ):
-    rows, cols = picked_ref.shape
+    rows, cols = pieces.shape[1:]
     minors = nd // nt
+    windows = rows // minors
+    held, depth = attended_ref.shape
+    tokens = held // windows
+    half = depth // 2
     me_t = lax.axis_index("tensor")
     me_d = lax.axis_index("dp")
     group = me_d // minors
     minor = me_d % minors
-
-    load = pltpu.make_async_copy(weight_hbm, weight, weight_sem)
-    load.start()
+    order = sorted(range(nt), key=lambda i: min(i, nt - i))
+
+    load_out = pltpu.make_async_copy(out_weight_hbm, out_weight, weight_sem.at[0])
+    load_draft = pltpu.make_async_copy(draft_weight_hbm, draft_weight, weight_sem.at[1])
+    load_out.start()
+    load_draft.start()
     barrier = pltpu.get_barrier_semaphore()
     for k in range(nt):
         for j in range(minors):
@@ -55,9 +83,79 @@
     for i in range(1, nt):
         peer = ((group + i) % nt * minors + minor, me_t)
         pl.semaphore_signal(barrier, inc=1, device_id=peer, device_id_type=MESH)
-    pieces[0] = picked_ref[...]
     pl.semaphore_wait(barrier, nt * minors - 1 + nt - 1)
-    load.wait()
+
+    def accepted_copy(k):
+        return pltpu.make_async_remote_copy(
+            src_ref=accepted_ref,
+            dst_ref=accepted_near,
+            send_sem=accepted_send.at[k - 1],
+            recv_sem=accepted_recv,
+            device_id=(me_d, (me_t + k) % nt),
+            device_id_type=MESH,
+        )
+
+    accepted_local = pltpu.make_async_copy(accepted_ref, accepted_near, accepted_recv)
+
+    @pl.when(me_t == group)
+    def _():
+        for k in range(1, nt):
+            accepted_copy(k).start()
+        accepted_local.start()
+
+    rows_all[pl.ds(pl.multiple_of(me_d * held, held), held), :] = attended_ref[...]
+
+    def pick(counts, count, table):
+        place = lax.broadcasted_iota(jnp.int32, (count, table.shape[0]), 1).astype(F32)
+        window = lax.broadcasted_iota(jnp.int32, (count, table.shape[0]), 0).astype(F32)
+        chosen = place == window * tokens + (counts - 1.0)
+        return jnp.dot(
+            jnp.where(chosen, 1.0, 0.0).astype(BF16), table, preferred_element_type=F32
+        )
+
+    accepted_local.wait()
+    near = accepted_near[pl.ds(pl.multiple_of(minor * windows, windows), windows), 0:1]
+    picked = pick(near, windows, attended_ref[...])
+    first[pl.ds(pl.multiple_of(me_d * 2 * windows, 2 * windows), 2 * windows), :] = (
+        jnp.concatenate([picked[:, :half], picked[:, half:]], axis=0).astype(BF16)
+    )
+
+    def block_of(ref, i, j, block):
+        source = (group + nt - i) % nt * minors + (minor + minors - j) % minors
+        return ref.at[pl.ds(pl.multiple_of(source * block, block), block)], source
+
+    def group_copy(ref, block, send, recv, i):
+        slot, source = block_of(ref, 0, 0, block)
+        return pltpu.make_async_remote_copy(
+            src_ref=slot,
+            dst_ref=slot,
+            send_sem=send.at[i - 1],
+            recv_sem=recv.at[source],
+            device_id=((group + i) % nt * minors + minor, me_t),
+            device_id_type=MESH,
+        )
+
+    def member_copy(ref, block, send, recv, i, j):
+        slot, source = block_of(ref, i, 0, block)
+        return pltpu.make_async_remote_copy(
+            src_ref=slot,
+            dst_ref=slot,
+            send_sem=send.at[i, j - 1],
+            recv_sem=recv.at[source],
+            device_id=(group * minors + (minor + j) % minors, me_t),
+            device_id_type=MESH,
+        )
+
+    def arrived(ref, block, recv, i, j):
+        slot, source = block_of(ref, i, j, block)
+        pltpu.make_async_copy(slot, slot, recv.at[source]).wait()
+
+    first_group = functools.partial(group_copy, first, 2 * windows, first_send, first_recv)
+    first_member = functools.partial(member_copy, first, 2 * windows, first_pass, first_recv)
+    first_arrived = functools.partial(arrived, first, 2 * windows, first_recv)
+    all_group = functools.partial(group_copy, rows_all, held, all_send, all_recv)
+    all_member = functools.partial(member_copy, rows_all, held, all_pass, all_recv)
+    all_arrived = functools.partial(arrived, rows_all, held, all_recv)
 
     def spread_copy(s, i):
         return pltpu.make_async_remote_copy(
@@ -103,7 +201,112 @@
             device_id_type=MESH,
         )
 
-    order = sorted(range(nt), key=lambda i: min(i, nt - i))
+    def summed(s):
+        for k in range(1, nt):
+            part_copy(s, k).start()
+        total = partial[pl.ds(pl.multiple_of(me_t * rows, rows), rows), :]
+        for k in range(1, nt):
+            part_copy(s, k).wait_recv()
+            total = total + landed[s, k - 1].astype(F32)
+        return total
+
+    for i in order[1:]:
+        first_group(i).start()
+    for i in order:
+        if i:
+            first_arrived(i, 0)
+        for j in range(1, minors):
+            first_member(i, j).start()
+    residual_picked = pick(accepted_ref[:, 0:1], rows, residual_ref[...])
+    load_out.wait()
+    for i in order:
+        for j in range(1, minors):
+            first_arrived(i, j)
+    for c in range(0, cols, 256):
+        low = jnp.dot(first[...], out_weight[:half, c : c + 256], preferred_element_type=F32)
+        high = jnp.dot(first[...], out_weight[half:, c : c + 256], preferred_element_type=F32)
+        product = (
+            low.reshape(nd, 2, windows, 256)[:, 0] + high.reshape(nd, 2, windows, 256)[:, 1]
+        ).reshape(nd * windows, 256)
+        partial[:, c : c + 256] = product
+        outgoing[STEPS, :, c : c + 256] = product.astype(BF16)
+    pieces[0] = (residual_picked + summed(STEPS)).astype(BF16)
+    load_draft.wait()
+
+    def rows_copy(i):
+        return pltpu.make_async_remote_copy(
+            src_ref=rows_out.at[i],
+            dst_ref=rows_in.at[me_t],
+            send_sem=rows_send.at[i],
+            recv_sem=rows_recv.at[me_t],
+            device_id=(me_d, (group + nt - i) % nt),
+            device_id_type=MESH,
+        )
+
+    def project(i):
+        for j in range(1, minors):
+            all_arrived(i, j)
+        target = (group + nt - i) % nt
+        span = minors * held
+        block = rows_all.at[pl.ds(pl.multiple_of(target * span, span), span)]
+        for c in range(0, cols, 256):
+            product = jnp.dot(block[...], out_weight[:, c : c + 256], preferred_element_type=F32)
+            rows_out[i, :, c : c + 256] = product.astype(BF16)
+
+            @pl.when(target == me_t)
+            def _():
+                rows_own[:, c : c + 256] = product
+
+        @pl.when(target != me_t)
+        def _():
+            rows_copy(i).start()
+
+    def forward(i):
+        all_arrived(i, 0)
+        for j in range(1, minors):
+            all_member(i, j).start()
+
+    def collect():
+        for k in range(1, nt):
+            source = (me_t + k) % nt
+            slot = rows_in.at[source]
+            pltpu.make_async_copy(slot, slot, rows_recv.at[source]).wait()
+        for c in range(0, cols, 256):
+            total = rows_own[:, c : c + 256] + residual_ref[:, c : c + 256].astype(F32)
+            for k in range(1, nt):
+                total = total + rows_in[(me_t + k) % nt, :, c : c + 256].astype(F32)
+            verified_ref[:, c : c + 256] = total.astype(BF16)
+
+    close = nt // 2 + 1
+
+    def background(s):
+        @pl.when(s == 0)
+        def _():
+            for i in order[1:]:
+                all_group(i).start()
+            for j in range(1, minors):
+                all_member(0, j).start()
+
+        @pl.when(s == 1)
+        def _():
+            project(order[0])
+            for i in order[1:close]:
+                forward(i)
+
+        @pl.when(s == 2)
+        def _():
+            project(order[1])
+            for i in order[close:]:
+                forward(i)
+
+        @pl.when(s == 3)
+        def _():
+            for i in order[2:]:
+                project(i)
+
+        @pl.when(s == STEPS - 1)
+        def _():
+            collect()
 
     def step(s, carry):
         for i in order[1:]:
@@ -123,6 +326,9 @@
             def _():
                 feat_local(s, i).start()
 
+            if i == 0:
+                background(s)
+
         for t in range(nt):
             for m in range(minors):
                 pltpu.make_async_copy(
@@ -132,18 +338,12 @@
                 ).wait()
         for c in range(0, cols, 256):
             product = jnp.dot(
-                feats[s], weight[:, c : c + 256], preferred_element_type=F32
+                feats[s], draft_weight[:, c : c + 256], preferred_element_type=F32
             )
             partial[:, c : c + 256] = product
             outgoing[s, :, c : c + 256] = product.astype(BF16)
-        for k in range(1, nt):
-            part_copy(s, k).start()
-        total = partial[pl.ds(pl.multiple_of(me_t * rows, rows), rows), :]
-        for k in range(1, nt):
-            part_copy(s, k).wait_recv()
-            total = total + landed[s, k - 1].astype(F32)
-        drafted = jnp.tanh(2.0 * total).astype(BF16)
-        out_ref[s] = drafted
+        drafted = jnp.tanh(2.0 * summed(s)).astype(BF16)
+        drafted_ref[s] = drafted
         pieces[s + 1] = drafted
         return carry
 
@@ -164,43 +364,84 @@
         return carry
 
     lax.fori_loop(0, STEPS, drain, 0)
-
-
-def draft(nt, nd, picked, draft_weight):
-    rows, cols = picked.shape
-    depth = draft_weight.shape[0]
+    for i in range(nt):
+        if i:
+            part_copy(STEPS, i).wait_send()
+            first_group(i).wait_send()
+            all_group(i).wait_send()
+        for j in range(1, minors):
+            first_member(i, j).wait_send()
+            all_member(i, j).wait_send()
+
+        @pl.when((group + nt - i) % nt != me_t)
+        def _():
+            rows_copy(i).wait_send()
+
+    @pl.when(me_t == group)
+    def _():
+        for k in range(1, nt):
+            accepted_copy(k).wait_send()
+
+
+def decode(nt, nd, attended, accepted, residual, out_weight, draft_weight):
+    held, depth = attended.shape
+    span, cols = residual.shape
+    rows = accepted.shape[0]
     minors = nd // nt
+    windows = rows // minors
     dma = pltpu.SemaphoreType.DMA
+    vmem = pl.BlockSpec(memory_space=pltpu.VMEM)
+    hbm = pl.BlockSpec(memory_space=pl.ANY)
     return pl.pallas_call(
-        functools.partial(draft_kernel, nt, nd),
-        out_shape=jax.ShapeDtypeStruct((STEPS, rows, cols), BF16),
-        in_specs=[pl.BlockSpec(memory_space=pltpu.VMEM), pl.BlockSpec(memory_space=pl.ANY)],
-        out_specs=pl.BlockSpec(memory_space=pltpu.VMEM),
+        functools.partial(decode_kernel, nt, nd),
+        out_shape=(
+            jax.ShapeDtypeStruct((span, cols), BF16),
+            jax.ShapeDtypeStruct((STEPS, rows, cols), BF16),
+        ),
+        in_specs=[vmem, vmem, vmem, hbm, hbm],
+        out_specs=(vmem, vmem),
         scratch_shapes=[
             pltpu.VMEM((depth, cols), BF16),
+            pltpu.VMEM((depth, cols), BF16),
+            pltpu.VMEM(accepted.shape, F32),
+            pltpu.VMEM((nd * 2 * windows, depth // 2), BF16),
             pltpu.VMEM((STEPS + 1, rows, cols), BF16),
             pltpu.VMEM((STEPS, nt - 1, rows, cols), BF16),
             pltpu.VMEM((STEPS, nt * rows, depth), BF16),
             pltpu.VMEM((nt * rows, cols), F32),
-            pltpu.VMEM((STEPS, nt * rows, cols), BF16),
-            pltpu.VMEM((STEPS, nt - 1, rows, cols), BF16),
+            pltpu.VMEM((STEPS + 1, nt * rows, cols), BF16),
+            pltpu.VMEM((STEPS + 1, nt - 1, rows, cols), BF16),
+            pltpu.VMEM((nd * held, depth), BF16),
+            pltpu.VMEM((span, cols), F32),
+            pltpu.VMEM((nt, span, cols), BF16),
+            pltpu.VMEM((nt, span, cols), BF16),
+            dma((2,)),
+            dma((nt - 1,)),
             dma,
+            dma((nt - 1,)),
+            dma((nt, minors - 1)),
+            dma((nd,)),
             dma((STEPS, nt - 1)),
             dma((STEPS, nt - 1)),
             dma((STEPS, nt, minors)),
             dma((STEPS, nt, minors)),
-            dma((STEPS, nt - 1)),
-            dma((STEPS, nt - 1)),
+            dma((STEPS + 1, nt - 1)),
+            dma((STEPS + 1, nt - 1)),
+            dma((nt - 1,)),
+            dma((nt, minors - 1)),
+            dma((nd,)),
+            dma((nt,)),
+            dma((nt,)),
         ],
         compiler_params=pltpu.CompilerParams(
-            collective_id=0, has_side_effects=True, vmem_limit_bytes=40 * 1024 * 1024
+            collective_id=0, has_side_effects=True, vmem_limit_bytes=48 * 1024 * 1024
         ),
         cost_estimate=pl.CostEstimate(
-            flops=2 * STEPS * nt * rows * depth * cols,
-            bytes_accessed=2 * depth * cols,
+            flops=2 * (STEPS * nt * rows + nd * held) * depth * cols,
+            bytes_accessed=4 * depth * cols,
             transcendentals=STEPS * rows * cols,
         ),
-    )(picked, draft_weight)
+    )(attended, accepted, residual, out_weight, draft_weight)
 
 
 def per_device(
@@ -255,27 +496,17 @@
         preferred_element_type=jnp.float32,
     )
     attended = mixed_rows.astype(jnp.bfloat16).reshape(windows_here * tokens_here, query_width)
-    partial_out = jnp.dot(
-        lax.all_gather(attended, "dp", axis=0, tiled=True),
+    block_windows, block_tokens, block_cols = residual.shape
+    verified, drafted = decode(
+        lax.axis_size("tensor"),
+        lax.axis_size("dp"),
+        attended,
+        jnp.broadcast_to(accepted.astype(F32)[:, None], (block_windows, HD)),
+        residual.reshape(block_windows * block_tokens, block_cols),
         out_weight,
-        preferred_element_type=jnp.float32,
-    )
-    summed = lax.psum_scatter(partial_out, "tensor", scatter_dimension=0, tiled=True)
-    block_windows, block_tokens, block_cols = residual.shape
-    flat_residual = residual.reshape(block_windows * block_tokens, block_cols).astype(jnp.float32)
-    verified = (
-        (flat_residual + summed)
-        .astype(jnp.bfloat16)
-        .reshape(block_windows, block_tokens, block_cols)
-    )
-    chosen = jnp.arange(block_tokens)[None, :] == (accepted - 1)[:, None]
-    picked = jnp.sum(
-        jnp.where(chosen[:, :, None], verified, jnp.zeros((), jnp.bfloat16)),
-        axis=1,
-        dtype=jnp.bfloat16,
-    )
-    drafted = draft(lax.axis_size("tensor"), lax.axis_size("dp"), picked, draft_weight)
-    return (verified, drafted)
+        draft_weight,
+    )
+    return (verified.reshape(residual.shape), drafted)
 
 
 def solution(mesh):

time: 170 us -> 113 us (0.66)
  waiting for transfers between devices: 72.5 us -> 0 us
  Pallas kernels: 63.6 us -> 99.6 us
  between operations: 14.2 us -> 0.8 us
  matrix products: 7.59 us -> 1.97 us
    all_gather x1 -> x0, waiting for transfers between devices: 47 us -> none  [per_device(): lax.all_gather(attended, 'dp', axis=0, tiled=True)]
    pallas_call x1, Pallas kernels: 63.6 us -> 99.6 us  [decode(): pl.pallas_call(functools.partial(decode_kernel, nt, nd), out_shape=(jax.S...]
    reduce_scatter x1 -> x0, waiting for transfers between devices: 25.5 us -> none  [per_device(): lax.psum_scatter(partial_out, 'tensor', scatter_dimension=0, tiled=True)]
    dot_general x1 -> x0, matrix products: 5.61 us -> none  [per_device(): jnp.dot(lax.all_gather(attended, 'dp', axis=0, tiled=True), out_weight, p...]
    unnamed x18 -> x19, local copies, waits for them, and re-layouts: 6.38 us -> 6.39 us
  transfers between devices with their start and end apart: 2 -> 0, of which waited for: 2 -> 0; matrix products, arithmetic and copies ran while one was open for 0% -> 0% of each run, Pallas kernels for 0% -> 0%
where the time goes in v2:
time: 113 us; the launch traced here: 112 us
  Pallas kernels  99.6 us (88%)
  local copies, waits for them, and re-layouts  8.97 us (8%)
  matrix products  1.97 us (2%)
    pallas_call x1, Pallas kernels, decode(): pl.pallas_call(functools.partial(decode_kernel, nt, nd), out_shape=(jax.S...  99.6 us
    unnamed x19, local copies, waits for them, and re-layouts  6.39 us

profile of v2, /device:TPU:0, one launch (start us, length us, event | category | flops | bytes accessed | tf_op | source)
XLA Modules:
  0.0 112.4 jit_solution(17682619467507684094)
XLA Ops:
  0.6 0.0 copy-start
  0.6 0.0 copy-start.6
  0.7 0.9 copy-done
  1.6 1.3 %reshape.52 = bf16[8,256,2,128]{3,2,1,0:T(2,128)(2,1)S(1)} reshape(bf16[8,256,256]{2,1,0:T(8,128)(2,1)} %param.13) | data formatting | bytes 2097152 | tf_op jit(solution)/shard_map/reshape | solution.py:464
  2.9 0.0 copy-done.6
  2.9 0.1 iota_compare_fusion
  3.0 0.0 copy-start.4
  3.0 0.5 fusion.17
  3.5 0.2 copy-done.4
  3.7 1.0 fusion.11
  4.7 0.2 fusion.16
  5.0 0.6 copy.60
  5.6 0.4 fusion.8
  6.0 0.0 copy-start.2
  6.0 0.3 divide_convert_fusion
  6.3 0.9 copy-done.2
  7.2 0.3 reshape.55
  7.5 0.0 copy-start.5
  7.5 0.3 fusion.5
  7.8 0.0 copy-start.3
  7.8 0.4 copy-done.5
  8.3 0.0 copy-start.7
  8.3 0.2 fusion.4
  8.5 0.1 reshape.57.attended_ref
  8.6 0.2 copy-done.3
  8.8 0.1 copy.65
  8.9 0.1 reshape.58.residual_ref
  9.0 0.0 copy-done.7
  9.0 0.1 broadcast_in_dim.37.accepted_ref
  9.0 0.0 copy-start.1
  9.0 2.2 %copy-done.1 = bf16[2048,1024]{1,0:T(8,128)(2,1)S(1)} copy-done((bf16[2048,1024]{1,0:T(8,128)(2,1)S(1)}, bf16[2048,1024]{1,0:T(8,128)(2,1)}, u32[]{:S(2)}) %copy-start.1) | copy-done | bytes 4194328
  11.2 99.6 %shard_map.113 = (bf16[96,1024]{1,0:T(8,128)(2,1)S(1)}, bf16[5,16,1024]{2,1,0:T(8,128)(2,1)S(1)}) custom-call(bf16[48,2048]{1,0:T(8,128)(2,1)S(1)} %reshape.57.attended_ref, f32[16,128]{1,0:T(8,128)S(1)} %broadcast_in_dim.37.accepted_ref, bf16[96,1024]{1,0:T(8,128)(2,1)S(1)} %reshape.58.residual_ref, bf16[2048,1024]{1,0:T(8,128)(2,1)S(1)} %copy-done.1, ...), custom_call_target="tpu_custom_call" | custom-call | flops 2952790016 | bytes 8388608 | tf_op jit(solution)/shard_map/pallas_call | solution.py:395
  110.8 0.1 reshape.59
  110.9 0.8 copy.66
  111.7 0.7 copy.101
  (4 shorter events, 0.1 us)
Async XLA Ops:
  0.6 0.9 copy-start
  0.6 2.3 %copy-start.6 = (s32[8]{0:T(128)S(1)}, s32[8]{0:T(128)}, u32[]{:S(2)}) copy-start(s32[8]{0:T(128)} %param.15) | copy-start | bytes 100
  3.0 0.7 copy-start.4
  6.0 1.2 %copy-start.2 = (bf16[8,256,256]{2,1,0:T(8,128)(2,1)S(1)}, bf16[8,256,256]{2,1,0:T(8,128)(2,1)}, u32[]{:S(2)}) copy-start(bf16[8,256,256]{2,1,0:T(8,128)(2,1)} %param.14) | copy-start | bytes 3145732
  7.5 0.7 copy-start.5
  7.8 0.9 copy-start.3
  8.3 0.7 copy-start.7
  9.0 2.2 %copy-start.1 = (bf16[2048,1024]{1,0:T(8,128)(2,1)S(1)}, bf16[2048,1024]{1,0:T(8,128)(2,1)}, u32[]{:S(2)}) copy-start(bf16[2048,1024]{1,0:T(8,128)(2,1)} %out_weight_hbm.1) | copy-start | bytes 12582916

commit v3 on v2

--- a/solution.py
+++ b/solution.py
@@ -9,6 +9,7 @@
 
 HD = 128
 STEPS = 5
+CUTS = 2
 
 
 MESH = pl.DeviceIdType.MESH
@@ -58,7 +59,9 @@
     rows_send,
     rows_recv,
 ):
-    rows, cols = pieces.shape[1:]
+    rows, part = pieces.shape[2:]
+    cols = part * CUTS
+    chunk = min(part, 256)
     minors = nd // nt
     windows = rows // minors
     held, depth = attended_ref.shape
@@ -69,6 +72,11 @@
     group = me_d // minors
     minor = me_d % minors
     order = sorted(range(nt), key=lambda i: min(i, nt - i))
+    spans = max(1, STEPS - 2)
+    turns = [
+        [i for q, i in enumerate(order[1:]) if q * spans // (nt - 1) == turn]
+        for turn in range(spans)
+    ]
 
     load_out = pltpu.make_async_copy(out_weight_hbm, out_weight, weight_sem.at[0])
     load_draft = pltpu.make_async_copy(draft_weight_hbm, draft_weight, weight_sem.at[1])
@@ -157,80 +165,113 @@
     all_member = functools.partial(member_copy, rows_all, held, all_pass, all_recv)
     all_arrived = functools.partial(arrived, rows_all, held, all_recv)
 
-    def spread_copy(s, i):
-        return pltpu.make_async_remote_copy(
-            src_ref=pieces.at[s],
-            dst_ref=spread.at[s, i - 1],
-            send_sem=spread_send.at[s, i - 1],
-            recv_sem=spread_recv.at[s, i - 1],
+    def spread_copy(s, h, i):
+        return pltpu.make_async_remote_copy(
+            src_ref=pieces.at[s, h],
+            dst_ref=spread.at[s, h, i - 1],
+            send_sem=spread_send.at[s, h, i - 1],
+            recv_sem=spread_recv.at[s, h, i - 1],
             device_id=((group + i) % nt * minors + minor, me_t),
             device_id_type=MESH,
         )
 
-    def feat_slot(s):
+    def feat_slot(s, h):
         return feats.at[
             s,
+            h,
             pl.ds(pl.multiple_of(me_t * rows, rows), rows),
-            pl.ds(pl.multiple_of(minor * cols, cols), cols),
+            pl.ds(pl.multiple_of(minor * part, part), part),
         ]
 
-    def feat_copy(s, i, j):
-        return pltpu.make_async_remote_copy(
-            src_ref=pieces.at[s] if i == 0 else spread.at[s, i - 1],
-            dst_ref=feat_slot(s),
-            send_sem=feat_send.at[s, i, j],
-            recv_sem=feat_recv.at[s, me_t, minor],
+    def feat_copy(s, h, i, j):
+        return pltpu.make_async_remote_copy(
+            src_ref=pieces.at[s, h] if i == 0 else spread.at[s, h, i - 1],
+            dst_ref=feat_slot(s, h),
+            send_sem=feat_send.at[s, h, i, j],
+            recv_sem=feat_recv.at[s, h, me_t, minor],
             device_id=(group * minors + (minor + j) % minors, (group + nt - i) % nt),
             device_id_type=MESH,
         )
 
-    def feat_local(s, i):
+    def feat_local(s, h, i):
         return pltpu.make_async_copy(
-            pieces.at[s] if i == 0 else spread.at[s, i - 1],
-            feat_slot(s),
-            feat_recv.at[s, me_t, minor],
-        )
-
-    def part_copy(s, k):
-        return pltpu.make_async_remote_copy(
-            src_ref=outgoing.at[s, pl.ds(pl.multiple_of((me_t + k) % nt * rows, rows), rows)],
-            dst_ref=landed.at[s, k - 1],
-            send_sem=part_send.at[s, k - 1],
-            recv_sem=part_recv.at[s, k - 1],
+            pieces.at[s, h] if i == 0 else spread.at[s, h, i - 1],
+            feat_slot(s, h),
+            feat_recv.at[s, h, me_t, minor],
+        )
+
+    def deliver(s, h, i):
+        target = (group + nt - i) % nt
+        for j in range(1, minors):
+            feat_copy(s, h, i, j).start()
+
+        @pl.when(target != me_t)
+        def _():
+            feat_copy(s, h, i, 0).start()
+
+        @pl.when(target == me_t)
+        def _():
+            feat_local(s, h, i).start()
+
+    def launch(s, h):
+        for i in order[1:]:
+            spread_copy(s, h, i).start()
+        deliver(s, h, 0)
+
+    def part_copy(s, n, k):
+        return pltpu.make_async_remote_copy(
+            src_ref=outgoing.at[s, n, pl.ds(pl.multiple_of((me_t + k) % nt * rows, rows), rows)],
+            dst_ref=landed.at[s, n, k - 1],
+            send_sem=part_send.at[s, n, k - 1],
+            recv_sem=part_recv.at[s, n, k - 1],
             device_id=(me_d, (me_t + k) % nt),
             device_id_type=MESH,
         )
 
-    def summed(s):
+    def share(s, n):
         for k in range(1, nt):
-            part_copy(s, k).start()
-        total = partial[pl.ds(pl.multiple_of(me_t * rows, rows), rows), :]
+            part_copy(s, n, k).start()
+
+    def summed(s, n):
+        total = partial[n, pl.ds(pl.multiple_of(me_t * rows, rows), rows), :]
         for k in range(1, nt):
-            part_copy(s, k).wait_recv()
-            total = total + landed[s, k - 1].astype(F32)
+            part_copy(s, n, k).wait_recv()
+            total = total + landed[s, n, k - 1].astype(F32)
         return total
 
     for i in order[1:]:
         first_group(i).start()
+    for j in range(1, minors):
+        all_member(0, j).start()
     for i in order:
         if i:
             first_arrived(i, 0)
         for j in range(1, minors):
             first_member(i, j).start()
+    for i in turns[0]:
+        all_group(i).start()
     residual_picked = pick(accepted_ref[:, 0:1], rows, residual_ref[...])
     load_out.wait()
     for i in order:
         for j in range(1, minors):
             first_arrived(i, j)
-    for c in range(0, cols, 256):
-        low = jnp.dot(first[...], out_weight[:half, c : c + 256], preferred_element_type=F32)
-        high = jnp.dot(first[...], out_weight[half:, c : c + 256], preferred_element_type=F32)
-        product = (
-            low.reshape(nd, 2, windows, 256)[:, 0] + high.reshape(nd, 2, windows, 256)[:, 1]
-        ).reshape(nd * windows, 256)
-        partial[:, c : c + 256] = product
-        outgoing[STEPS, :, c : c + 256] = product.astype(BF16)
-    pieces[0] = (residual_picked + summed(STEPS)).astype(BF16)
+    for n in range(CUTS):
+        for c in range(0, part, chunk):
+            lanes = pl.ds(n * part + c, chunk)
+            low = jnp.dot(first[...], out_weight[:half, lanes], preferred_element_type=F32)
+            high = jnp.dot(first[...], out_weight[half:, lanes], preferred_element_type=F32)
+            product = (
+                low.reshape(nd, 2, windows, chunk)[:, 0]
+                + high.reshape(nd, 2, windows, chunk)[:, 1]
+            ).reshape(nd * windows, chunk)
+            partial[n, :, c : c + chunk] = product
+            outgoing[STEPS, n, :, c : c + chunk] = product.astype(BF16)
+        share(STEPS, n)
+    for n in range(CUTS):
+        pieces[0, n] = (
+            residual_picked[:, n * part : (n + 1) * part] + summed(STEPS, n)
+        ).astype(BF16)
+        launch(0, n)
     load_draft.wait()
 
     def rows_copy(i):
@@ -277,96 +318,95 @@
                 total = total + rows_in[(me_t + k) % nt, :, c : c + 256].astype(F32)
             verified_ref[:, c : c + 256] = total.astype(BF16)
 
-    close = nt // 2 + 1
-
-    def background(s):
-        @pl.when(s == 0)
-        def _():
-            for i in order[1:]:
-                all_group(i).start()
-            for j in range(1, minors):
-                all_member(0, j).start()
-
-        @pl.when(s == 1)
-        def _():
-            project(order[0])
-            for i in order[1:close]:
-                forward(i)
-
-        @pl.when(s == 2)
-        def _():
-            project(order[1])
-            for i in order[close:]:
-                forward(i)
-
-        @pl.when(s == 3)
-        def _():
-            for i in order[2:]:
-                project(i)
-
-        @pl.when(s == STEPS - 1)
+    def early(s):
+        for turn in range(spans + 1):
+
+            @pl.when(s == turn)
+            def _(turn=turn):
+                for i in turns[turn] if turn < spans else []:
+                    forward(i)
+                for i in turns[turn - 1] if turn else order[:1]:
+                    project(i)
+
+        @pl.when(s == spans + 1)
         def _():
             collect()
 
+    def late(s):
+        for turn in range(1, spans):
+
+            @pl.when(s == turn - 1)
+            def _(turn=turn):
+                for i in turns[turn]:
+                    all_group(i).start()
+
     def step(s, carry):
-        for i in order[1:]:
-            spread_copy(s, i).start()
-        for i in order:
-            if i:
-                spread_copy(s, i).wait_recv()
-            target = (group + nt - i) % nt
-            for j in range(1, minors):
-                feat_copy(s, i, j).start()
-
-            @pl.when(target != me_t)
+        early(s)
+        for h in range(CUTS):
+            for i in order[1:]:
+                spread_copy(s, h, i).wait_recv()
+                deliver(s, h, i)
+        late(s)
+        for h in range(CUTS):
+            for t in range(nt):
+                for m in range(minors):
+                    pltpu.make_async_copy(
+                        pieces.at[s, h],
+                        feats.at[s, h, pl.ds(t * rows, rows), pl.ds(m * part, part)],
+                        feat_recv.at[s, h, t, m],
+                    ).wait()
+            for n in range(CUTS):
+                for c in range(0, part, chunk):
+                    product = sum(
+                        jnp.dot(
+                            feats[s, h, :, m * part : (m + 1) * part],
+                            draft_weight[
+                                pl.ds(m * cols + h * part, part), pl.ds(n * part + c, chunk)
+                            ],
+                            preferred_element_type=F32,
+                        )
+                        for m in range(minors)
+                    )
+                    if h:
+                        product = product + partial[n, :, c : c + chunk]
+                    partial[n, :, c : c + chunk] = product
+                    if h == CUTS - 1:
+                        outgoing[s, n, :, c : c + chunk] = product.astype(BF16)
+                if h == CUTS - 1:
+                    share(s, n)
+        for n in range(CUTS):
+            drafted = jnp.tanh(2.0 * summed(s, n)).astype(BF16)
+            drafted_ref[s, :, n * part : (n + 1) * part] = drafted
+            pieces[s + 1, n] = drafted
+
+            @pl.when(s < STEPS - 1)
             def _():
-                feat_copy(s, i, 0).start()
-
-            @pl.when(target == me_t)
-            def _():
-                feat_local(s, i).start()
-
-            if i == 0:
-                background(s)
-
-        for t in range(nt):
-            for m in range(minors):
-                pltpu.make_async_copy(
-                    pieces.at[s],
-                    feats.at[s, pl.ds(t * rows, rows), pl.ds(m * cols, cols)],
-                    feat_recv.at[s, t, m],
-                ).wait()
-        for c in range(0, cols, 256):
-            product = jnp.dot(
-                feats[s], draft_weight[:, c : c + 256], preferred_element_type=F32
-            )
-            partial[:, c : c + 256] = product
-            outgoing[s, :, c : c + 256] = product.astype(BF16)
-        drafted = jnp.tanh(2.0 * summed(s)).astype(BF16)
-        drafted_ref[s] = drafted
-        pieces[s + 1] = drafted
+                launch(s + 1, n)
+
         return carry
 
     lax.fori_loop(0, STEPS, step, 0)
 
     def drain(s, carry):
-        for i in range(nt):
-            if i:
-                spread_copy(s, i).wait_send()
-                part_copy(s, i).wait_send()
-            for j in range(1, minors):
-                feat_copy(s, i, j).wait_send()
-
-            @pl.when((group + nt - i) % nt != me_t)
-            def _():
-                feat_copy(s, i, 0).wait_send()
+        for h in range(CUTS):
+            for i in range(nt):
+                if i:
+                    spread_copy(s, h, i).wait_send()
+                    part_copy(s, h, i).wait_send()
+                for j in range(1, minors):
+                    feat_copy(s, h, i, j).wait_send()
+
+                @pl.when((group + nt - i) % nt != me_t)
+                def _():
+                    feat_copy(s, h, i, 0).wait_send()
 
         return carry
 
     lax.fori_loop(0, STEPS, drain, 0)
     for i in range(nt):
         if i:
-            part_copy(STEPS, i).wait_send()
+            for n in range(CUTS):
+                part_copy(STEPS, n, i).wait_send()
             first_group(i).wait_send()
             all_group(i).wait_send()
         for j in range(1, minors):
@@ -389,9 +429,10 @@
     rows = accepted.shape[0]
     minors = nd // nt
     windows = rows // minors
+    part = cols // CUTS
     dma = pltpu.SemaphoreType.DMA
     vmem = pl.BlockSpec(memory_space=pltpu.VMEM)
-    hbm = pl.BlockSpec(memory_space=pl.ANY)
+    hbm = pl.BlockSpec(memory_space=pltpu.HBM)
     return pl.pallas_call(
         functools.partial(decode_kernel, nt, nd),
         out_shape=(
@@ -405,12 +446,12 @@
             pltpu.VMEM((depth, cols), BF16),
             pltpu.VMEM(accepted.shape, F32),
             pltpu.VMEM((nd * 2 * windows, depth // 2), BF16),
-            pltpu.VMEM((STEPS + 1, rows, cols), BF16),
-            pltpu.VMEM((STEPS, nt - 1, rows, cols), BF16),
-            pltpu.VMEM((STEPS, nt * rows, depth), BF16),
-            pltpu.VMEM((nt * rows, cols), F32),
-            pltpu.VMEM((STEPS + 1, nt * rows, cols), BF16),
-            pltpu.VMEM((STEPS + 1, nt - 1, rows, cols), BF16),
+            pltpu.VMEM((STEPS + 1, CUTS, rows, part), BF16),
+            pltpu.VMEM((STEPS, CUTS, nt - 1, rows, part), BF16),
+            pltpu.VMEM((STEPS, CUTS, nt * rows, minors * part), BF16),
+            pltpu.VMEM((CUTS, nt * rows, part), F32),
+            pltpu.VMEM((STEPS + 1, CUTS, nt * rows, part), BF16),
+            pltpu.VMEM((STEPS + 1, CUTS, nt - 1, rows, part), BF16),
             pltpu.VMEM((nd * held, depth), BF16),
             pltpu.VMEM((span, cols), F32),
             pltpu.VMEM((nt, span, cols), BF16),
@@ -421,12 +462,12 @@
             dma((nt - 1,)),
             dma((nt, minors - 1)),
             dma((nd,)),
-            dma((STEPS, nt - 1)),
-            dma((STEPS, nt - 1)),
-            dma((STEPS, nt, minors)),
-            dma((STEPS, nt, minors)),
-            dma((STEPS + 1, nt - 1)),
-            dma((STEPS + 1, nt - 1)),
+            dma((STEPS, CUTS, nt - 1)),
+            dma((STEPS, CUTS, nt - 1)),
+            dma((STEPS, CUTS, nt, minors)),
+            dma((STEPS, CUTS, nt, minors)),
+            dma((STEPS + 1, CUTS, nt - 1)),
+            dma((STEPS + 1, CUTS, nt - 1)),
             dma((nt - 1,)),
             dma((nt, minors - 1)),
             dma((nd,)),

time: 113 us -> 104 us (0.920)
  Pallas kernels: 99.6 us -> 90.5 us
    pallas_call x1, Pallas kernels: 99.6 us -> 90.5 us  [decode(): pl.pallas_call(functools.partial(decode_kernel, nt, nd), out_shape=(jax.S...]
where the time goes in v3:
time: 104 us; the launch traced here: 103 us
  Pallas kernels  90.5 us (87%)
  local copies, waits for them, and re-layouts  8.97 us (9%)
  matrix products  1.97 us (2%)
  other arithmetic  1.04 us (1%)
    pallas_call x1, Pallas kernels, decode(): pl.pallas_call(functools.partial(decode_kernel, nt, nd), out_shape=(jax.S...  90.5 us
    unnamed x19, local copies, waits for them, and re-layouts  6.39 us

profile of v3, /device:TPU:0, one launch (start us, length us, event | category | flops | bytes accessed | tf_op | source)
XLA Modules:
  0.0 103.3 jit_solution(206999662207966769)
XLA Ops:
  0.6 0.0 copy-start
  0.6 0.0 copy-start.6
  0.7 0.9 copy-done
  1.6 1.3 %reshape.52 = bf16[8,256,2,128]{3,2,1,0:T(2,128)(2,1)S(1)} reshape(bf16[8,256,256]{2,1,0:T(8,128)(2,1)} %param.13) | data formatting | bytes 2097152 | tf_op jit(solution)/shard_map/reshape | solution.py:505
  2.9 0.0 copy-done.6
  2.9 0.1 iota_compare_fusion
  3.0 0.0 copy-start.4
  3.0 0.5 fusion.17
  3.5 0.2 copy-done.4
  3.7 1.0 fusion.11
  4.7 0.2 fusion.16
  5.0 0.6 copy.60
  5.6 0.4 fusion.8
  6.0 0.0 copy-start.2
  6.0 0.3 divide_convert_fusion
  6.3 0.9 copy-done.2
  7.2 0.3 reshape.55
  7.5 0.0 copy-start.5
  7.5 0.3 fusion.5
  7.8 0.0 copy-start.3
  7.8 0.4 copy-done.5
  8.3 0.0 copy-start.7
  8.3 0.2 fusion.4
  8.5 0.1 reshape.57.attended_ref
  8.6 0.2 copy-done.3
  8.8 0.1 copy.65
  8.9 0.1 reshape.58.residual_ref
  9.0 0.0 copy-done.7
  9.0 0.1 broadcast_in_dim.37.accepted_ref
  9.0 0.0 copy-start.1
  9.0 2.2 %copy-done.1 = bf16[2048,1024]{1,0:T(8,128)(2,1)S(1)} copy-done((bf16[2048,1024]{1,0:T(8,128)(2,1)S(1)}, bf16[2048,1024]{1,0:T(8,128)(2,1)}, u32[]{:S(2)}) %copy-start.1) | copy-done | bytes 4194328
  11.2 90.5 %shard_map.113 = (bf16[96,1024]{1,0:T(8,128)(2,1)S(1)}, bf16[5,16,1024]{2,1,0:T(8,128)(2,1)S(1)}) custom-call(bf16[48,2048]{1,0:T(8,128)(2,1)S(1)} %reshape.57.attended_ref, f32[16,128]{1,0:T(8,128)S(1)} %broadcast_in_dim.37.accepted_ref, bf16[96,1024]{1,0:T(8,128)(2,1)S(1)} %reshape.58.residual_ref, bf16[2048,1024]{1,0:T(8,128)(2,1)S(1)} %copy-done.1, ...), custom_call_target="tpu_custom_call" | custom-call | flops 2952790016 | bytes 8388608 | tf_op jit(solution)/shard_map/pallas_call | solution.py:436
  101.8 0.1 reshape.59
  101.8 0.8 copy.66
  102.6 0.7 copy.101
  (4 shorter events, 0.1 us)
Async XLA Ops:
  0.6 0.9 copy-start
  0.6 2.3 %copy-start.6 = (s32[8]{0:T(128)S(1)}, s32[8]{0:T(128)}, u32[]{:S(2)}) copy-start(s32[8]{0:T(128)} %param.15) | copy-start | bytes 100
  3.0 0.7 copy-start.4
  6.0 1.2 %copy-start.2 = (bf16[8,256,256]{2,1,0:T(8,128)(2,1)S(1)}, bf16[8,256,256]{2,1,0:T(8,128)(2,1)}, u32[]{:S(2)}) copy-start(bf16[8,256,256]{2,1,0:T(8,128)(2,1)} %param.14) | copy-start | bytes 3145732
  7.5 0.7 copy-start.5
  7.8 0.9 copy-start.3
  8.3 0.7 copy-start.7
  9.0 2.2 %copy-start.1 = (bf16[2048,1024]{1,0:T(8,128)(2,1)S(1)}, bf16[2048,1024]{1,0:T(8,128)(2,1)}, u32[]{:S(2)}) copy-start(bf16[2048,1024]{1,0:T(8,128)(2,1)} %out_weight_hbm.1) | copy-start | bytes 12582916

commit v4 on v3

--- a/solution.py
+++ b/solution.py
@@ -20,15 +20,26 @@
 def decode_kernel(
     nt,
     nd,
-    attended_ref,
+    queries_ref,
+    new_keys_ref,
+    new_values_ref,
+    lengths_ref,
     accepted_ref,
     residual_ref,
+    key_cache_hbm,
+    value_cache_hbm,
     out_weight_hbm,
     draft_weight_hbm,
     verified_ref,
     drafted_ref,
     out_weight,
     draft_weight,
+    keys,
+    values,
+    query_pad,
+    key_pad,
+    value_pad,
+    mixed,
     accepted_near,
     first,
     pieces,
@@ -63,9 +74,11 @@
     cols = part * CUTS
     chunk = min(part, 256)
     minors = nd // nt
-    windows = rows // minors
-    held, depth = attended_ref.shape
-    tokens = held // windows
+    windows, tokens, depth = queries_ref.shape
+    held = windows * tokens
+    cache = key_cache_hbm.shape[1]
+    slots, kv_width = keys.shape[1:]
+    token_pad = query_pad.shape[1]
     half = depth // 2
     me_t = lax.axis_index("tensor")
     me_d = lax.axis_index("dp")
@@ -80,6 +93,14 @@
 
     load_out = pltpu.make_async_copy(out_weight_hbm, out_weight, weight_sem.at[0])
     load_draft = pltpu.make_async_copy(draft_weight_hbm, draft_weight, weight_sem.at[1])
+    load_keys = pltpu.make_async_copy(
+        key_cache_hbm, keys.at[:, pl.ds(0, cache)], weight_sem.at[2]
+    )
+    load_values = pltpu.make_async_copy(
+        value_cache_hbm, values.at[:, pl.ds(0, cache)], weight_sem.at[3]
+    )
+    load_keys.start()
+    load_values.start()
     load_out.start()
     load_draft.start()
     barrier = pltpu.get_barrier_semaphore()
@@ -91,6 +112,61 @@
     for i in range(1, nt):
         peer = ((group + i) % nt * minors + minor, me_t)
         pl.semaphore_signal(barrier, inc=1, device_id=peer, device_id_type=MESH)
+
+    query_pad[...] = jnp.zeros_like(query_pad)
+    key_pad[...] = jnp.zeros_like(key_pad)
+    value_pad[...] = jnp.zeros_like(value_pad)
+    query_pad[:, :tokens, :] = queries_ref[...].astype(F32)
+    key_pad[:, :tokens, :] = new_keys_ref[...].astype(F32)
+    value_pad[:, :tokens, :] = new_values_ref[...].astype(F32)
+    keys[:, cache:, :] = key_pad[...].astype(BF16)
+    values[:, cache:, :] = value_pad[...].astype(BF16)
+    kv_heads = kv_width // HD
+    share_heads = depth // kv_width
+    query_rows = share_heads * token_pad
+    spot = lax.broadcasted_iota(jnp.int32, (query_rows, slots), 1)
+    token = lax.broadcasted_iota(jnp.int32, (query_rows, slots), 0) % token_pad
+    fresh_live = (spot >= cache) & (spot - cache <= token)
+    spot_float = spot.astype(F32)
+
+    def attend(chosen_windows):
+        units = [(w, k) for w in chosen_windows for k in range(kv_heads)]
+        scores = []
+        for w, k in units:
+            heads = [
+                query_pad[w, :, (k * share_heads + h) * HD : (k * share_heads + h + 1) * HD]
+                for h in range(share_heads)
+            ]
+            scores.append(
+                lax.dot_general(
+                    jnp.concatenate(heads, axis=0).astype(BF16),
+                    keys[w, :, k * HD : (k + 1) * HD],
+                    (((1,), (1,)), ((), ())),
+                    preferred_element_type=F32,
+                )
+                * HD ** (-0.5)
+            )
+        weights = []
+        for (w, _), score in zip(units, scores):
+            cached = (spot < cache) & (spot_float < lengths_ref[w : w + 1, 0:1])
+            score = jnp.where(cached | fresh_live, score, -1e30)
+            powered = jnp.exp(score - jnp.max(score, axis=-1, keepdims=True))
+            weights.append(
+                (powered * (1.0 / jnp.sum(powered, axis=-1, keepdims=True))).astype(BF16)
+            )
+        for (w, k), weight in zip(units, weights):
+            result = jnp.dot(
+                weight, values[w, :, k * HD : (k + 1) * HD], preferred_element_type=F32
+            )
+            for h in range(share_heads):
+                head = k * share_heads + h
+                mixed[w * token_pad : (w + 1) * token_pad, head * HD : (head + 1) * HD] = result[
+                    h * token_pad : (h + 1) * token_pad
+                ]
+
+    load_keys.wait()
+    load_values.wait()
+    attend(range(windows // 2))
     pl.semaphore_wait(barrier, nt * minors - 1 + nt - 1)
 
     def accepted_copy(k):
@@ -111,9 +187,10 @@
             accepted_copy(k).start()
         accepted_local.start()
 
-    rows_all[pl.ds(pl.multiple_of(me_d * held, held), held), :] = attended_ref[...]
-
-    def pick(counts, count, table):
+    attend(range(windows // 2, windows))
+    attended = mixed[...].astype(BF16)
+
+    def pick(counts, count, table, tokens):
         place = lax.broadcasted_iota(jnp.int32, (count, table.shape[0]), 1).astype(F32)
         window = lax.broadcasted_iota(jnp.int32, (count, table.shape[0]), 0).astype(F32)
         chosen = place == window * tokens + (counts - 1.0)
@@ -123,7 +200,7 @@
 
     accepted_local.wait()
     near = accepted_near[pl.ds(pl.multiple_of(minor * windows, windows), windows), 0:1]
-    picked = pick(near, windows, attended_ref[...])
+    picked = pick(near, windows, attended, token_pad)
     first[pl.ds(pl.multiple_of(me_d * 2 * windows, 2 * windows), 2 * windows), :] = (
         jnp.concatenate([picked[:, :half], picked[:, half:]], axis=0).astype(BF16)
     )
@@ -241,6 +318,12 @@
 
     for i in order[1:]:
         first_group(i).start()
+    place = lax.broadcasted_iota(jnp.int32, (held, windows * token_pad), 1)
+    row = lax.broadcasted_iota(jnp.int32, (held, windows * token_pad), 0)
+    compact = place == row // tokens * token_pad + row % tokens
+    rows_all[pl.ds(pl.multiple_of(me_d * held, held), held), :] = jnp.dot(
+        jnp.where(compact, 1.0, 0.0).astype(BF16), attended, preferred_element_type=F32
+    ).astype(BF16)
     for j in range(1, minors):
         all_member(0, j).start()
     for i in order:
@@ -250,7 +333,7 @@
             first_member(i, j).start()
     for i in turns[0]:
         all_group(i).start()
-    residual_picked = pick(accepted_ref[:, 0:1], rows, residual_ref[...])
+    residual_picked = pick(accepted_ref[:, 0:1], rows, residual_ref[...], tokens)
     load_out.wait()
     for i in order:
         for j in range(1, minors):
@@ -423,12 +506,15 @@
             accepted_copy(k).wait_send()
 
 
-def decode(nt, nd, attended, accepted, residual, out_weight, draft_weight):
-    held, depth = attended.shape
+def decode(nt, nd, queries, new_keys, new_values, lengths, accepted, residual, *large):
+    windows, tokens, depth = queries.shape
+    held = windows * tokens
     span, cols = residual.shape
     rows = accepted.shape[0]
+    cache, kv_width = large[0].shape[1:]
+    token_pad = -(-tokens // 8) * 8
+    fresh_pad = -(-tokens // 16) * 16
     minors = nd // nt
-    windows = rows // minors
     part = cols // CUTS
     dma = pltpu.SemaphoreType.DMA
     vmem = pl.BlockSpec(memory_space=pltpu.VMEM)
@@ -439,11 +525,17 @@
             jax.ShapeDtypeStruct((span, cols), BF16),
             jax.ShapeDtypeStruct((STEPS, rows, cols), BF16),
         ),
-        in_specs=[vmem, vmem, vmem, hbm, hbm],
+        in_specs=[vmem] * 6 + [hbm] * 4,
         out_specs=(vmem, vmem),
         scratch_shapes=[
             pltpu.VMEM((depth, cols), BF16),
             pltpu.VMEM((depth, cols), BF16),
+            pltpu.VMEM((windows, cache + fresh_pad, kv_width), BF16),
+            pltpu.VMEM((windows, cache + fresh_pad, kv_width), BF16),
+            pltpu.VMEM((windows, token_pad, depth), F32),
+            pltpu.VMEM((windows, fresh_pad, kv_width), F32),
+            pltpu.VMEM((windows, fresh_pad, kv_width), F32),
+            pltpu.VMEM((windows * token_pad, depth), F32),
             pltpu.VMEM(accepted.shape, F32),
             pltpu.VMEM((nd * 2 * windows, depth // 2), BF16),
             pltpu.VMEM((STEPS + 1, CUTS, rows, part), BF16),
@@ -456,7 +548,7 @@
             pltpu.VMEM((span, cols), F32),
             pltpu.VMEM((nt, span, cols), BF16),
             pltpu.VMEM((nt, span, cols), BF16),
-            dma((2,)),
+            dma((4,)),
             dma((nt - 1,)),
             dma,
             dma((nt - 1,)),
@@ -482,7 +574,7 @@
             bytes_accessed=4 * depth * cols,
             transcendentals=STEPS * rows * cols,
         ),
-    )(attended, accepted, residual, out_weight, draft_weight)
+    )(queries, new_keys, new_values, lengths, accepted, residual, *large)
 
 
 def per_device(
@@ -497,53 +589,18 @@
     out_weight,
     draft_weight,
 ):
-    windows_here, tokens_here, query_width = queries.shape
-    cache_size = key_cache.shape[1]
-    kv_here = new_keys.shape[2] // HD
-    group_size = query_width // HD // kv_here
-    query_split = queries.reshape(windows_here, tokens_here, kv_here, group_size, HD)
-    keys_cached = key_cache.reshape(windows_here, cache_size, kv_here, HD)
-    keys_fresh = new_keys.reshape(windows_here, tokens_here, kv_here, HD)
-    score_cache = jnp.einsum(
-        "wtkgd,wpkd->wkgtp", query_split, keys_cached, preferred_element_type=jnp.float32
-    ) * HD ** (-0.5)
-    score_fresh = jnp.einsum(
-        "wtkgd,wpkd->wkgtp", query_split, keys_fresh, preferred_element_type=jnp.float32
-    ) * HD ** (-0.5)
-    live_cache = (jnp.arange(cache_size)[None, :] < cache_lengths[:, None])[:, None, None, None, :]
-    live_fresh = jnp.arange(tokens_here)[None, :] <= jnp.arange(tokens_here)[:, None]
-    scores = jnp.concatenate(
-        [
-            jnp.where(live_cache, score_cache, -jnp.inf),
-            jnp.where(live_fresh, score_fresh, -jnp.inf),
-        ],
-        axis=-1,
-    )
-    largest = jnp.max(scores, axis=-1, keepdims=True)
-    powered = jnp.exp(scores - largest)
-    weights = (powered / jnp.sum(powered, axis=-1, keepdims=True)).astype(jnp.bfloat16)
-    values_cached = value_cache.reshape(windows_here, cache_size, kv_here, HD)
-    values_fresh = new_values.reshape(windows_here, tokens_here, kv_here, HD)
-    mixed_rows = jnp.einsum(
-        "wkgtp,wpkd->wtkgd",
-        weights[..., :cache_size],
-        values_cached,
-        preferred_element_type=jnp.float32,
-    )
-    mixed_rows = mixed_rows + jnp.einsum(
-        "wkgtp,wpkd->wtkgd",
-        weights[..., cache_size:],
-        values_fresh,
-        preferred_element_type=jnp.float32,
-    )
-    attended = mixed_rows.astype(jnp.bfloat16).reshape(windows_here * tokens_here, query_width)
     block_windows, block_tokens, block_cols = residual.shape
     verified, drafted = decode(
         lax.axis_size("tensor"),
         lax.axis_size("dp"),
-        attended,
+        queries,
+        new_keys,
+        new_values,
+        jnp.broadcast_to(cache_lengths.astype(F32)[:, None], (cache_lengths.shape[0], HD)),
         jnp.broadcast_to(accepted.astype(F32)[:, None], (block_windows, HD)),
         residual.reshape(block_windows * block_tokens, block_cols),
+        key_cache,
+        value_cache,
         out_weight,
         draft_weight,
     )

time: 104 us -> 100 us (0.962)
  matrix products: 1.97 us -> 0 us
  local copies, waits for them, and re-layouts: 8.97 us -> 7.76 us
    dot_general x4 -> x0, matrix products: 1.97 us -> none  [the longest x1 0.96 us: per_device(): jnp.einsum('wtkgd,wpkd->wkgtp', query_split, keys_fresh, preferred_elemen...]
    reshape x3 -> x0, local copies, waits for them, and re-layouts: 1.7 us -> none  [the longest x1 1.34 us: per_device(): keys_cached = key_cache.reshape(windows_here, cache_size, kv_here, HD)]
    unnamed x19 -> x10, local copies, waits for them, and re-layouts: 6.39 us -> 7.48 us
where the time goes in v4:
time: 100 us; the launch traced here: 99.7 us
  Pallas kernels  90 us (90%)
  local copies, waits for them, and re-layouts  7.76 us (8%)
  other arithmetic  1.32 us (1%)
    pallas_call x1, Pallas kernels, decode(): pl.pallas_call(functools.partial(decode_kernel, nt, nd), out_shape=(jax.S...  90 us
    unnamed x10, local copies, waits for them, and re-layouts  7.48 us

profile of v4, /device:TPU:0, one launch (start us, length us, event | category | flops | bytes accessed | tf_op | source)
XLA Modules:
  0.0 99.7 jit_solution(7212369059864866980)
XLA Ops:
  0.6 0.7 convert_element_type.6
  1.3 0.7 convert_element_type.7
  1.9 0.1 broadcast_in_dim.4.lengths_ref
  2.0 0.1 broadcast_in_dim.5.accepted_ref
  2.1 0.7 copy.19.new_keys_ref
  2.8 0.7 copy.20.new_values_ref
  3.6 1.0 %copy.18.queries_ref = bf16[8,6,2048]{2,1,0:T(8,128)(2,1)S(1)} copy(bf16[8,6,2048]{2,0,1:T(8,128)(2,1)} %param.10) | data formatting | bytes 393216 | tf_op args[0]
  4.6 1.0 %copy.17 = bf16[16,6,1024]{2,1,0:T(8,128)(2,1)S(1)} copy(bf16[16,6,1024]{2,0,1:T(8,128)(2,1)} %param.17) | data formatting | bytes 393216 | tf_op args[7]
  5.7 0.1 reshape.12.residual_ref
  5.7 0.0 copy-start
  5.8 1.2 %copy-done = bf16[8,256,256]{2,1,0:T(8,128)(2,1)S(1)} copy-done((bf16[8,256,256]{2,1,0:T(8,128)(2,1)S(1)}, bf16[8,256,256]{2,1,0:T(8,128)(2,1)}, u32[]{:S(2)}) %copy-start) | copy-done | bytes 1048600
  7.0 0.0 copy-start.1
  7.0 1.2 %copy-done.1 = bf16[8,256,256]{2,1,0:T(8,128)(2,1)S(1)} copy-done((bf16[8,256,256]{2,1,0:T(8,128)(2,1)S(1)}, bf16[8,256,256]{2,1,0:T(8,128)(2,1)}, u32[]{:S(2)}) %copy-start.1) | copy-done | bytes 1048600
  8.2 90.0 %shard_map.113 = (bf16[96,1024]{1,0:T(8,128)(2,1)S(1)}, bf16[5,16,1024]{2,1,0:T(8,128)(2,1)S(1)}) custom-call(bf16[8,6,2048]{2,1,0:T(8,128)(2,1)S(1)} %copy.18.queries_ref, bf16[8,6,256]{2,1,0:T(8,128)(2,1)S(1)} %copy.19.new_keys_ref, bf16[8,6,256]{2,1,0:T(8,128)(2,1)S(1)} %copy.20.new_values_ref, f32[8,128]{1,0:T(8,128)S(1)} %broadcast_in_dim.4.lengths_ref, ...), custom_call_target="tpu_custom_call" | custom-call | flops 2952790016 | bytes 8388608 | tf_op jit(solution)/shard_map/pallas_call | solution.py:522
  98.2 0.1 reshape.13
  98.3 0.8 copy.21
  99.0 0.7 copy.23
Async XLA Ops:
  5.7 1.2 %copy-start = (bf16[8,256,256]{2,1,0:T(8,128)(2,1)S(1)}, bf16[8,256,256]{2,1,0:T(8,128)(2,1)}, u32[]{:S(2)}) copy-start(bf16[8,256,256]{2,1,0:T(8,128)(2,1)} %key_cache_hbm.1) | copy-start | bytes 3145732
  7.0 1.2 %copy-start.1 = (bf16[8,256,256]{2,1,0:T(8,128)(2,1)S(1)}, bf16[8,256,256]{2,1,0:T(8,128)(2,1)}, u32[]{:S(2)}) copy-start(bf16[8,256,256]{2,1,0:T(8,128)(2,1)} %value_cache_hbm.1) | copy-start | bytes 3145732

commit v5 on v4

--- a/solution.py
+++ b/solution.py
@@ -37,8 +37,6 @@
     keys,
     values,
     query_pad,
-    key_pad,
-    value_pad,
     mixed,
     accepted_near,
     first,
@@ -74,11 +72,11 @@
     cols = part * CUTS
     chunk = min(part, 256)
     minors = nd // nt
-    windows, tokens, depth = queries_ref.shape
-    held = windows * tokens
-    cache = key_cache_hbm.shape[1]
-    slots, kv_width = keys.shape[1:]
-    token_pad = query_pad.shape[1]
+    held, depth = queries_ref.shape
+    windows, cache, kv_width = key_cache_hbm.shape
+    tokens = held // windows
+    slots = keys.shape[1]
+    token_pad = mixed.shape[0] // windows
     half = depth // 2
     me_t = lax.axis_index("tensor")
     me_d = lax.axis_index("dp")
@@ -113,21 +111,27 @@
         peer = ((group + i) % nt * minors + minor, me_t)
         pl.semaphore_signal(barrier, inc=1, device_id=peer, device_id_type=MESH)
 
-    query_pad[...] = jnp.zeros_like(query_pad)
-    key_pad[...] = jnp.zeros_like(key_pad)
-    value_pad[...] = jnp.zeros_like(value_pad)
-    query_pad[:, :tokens, :] = queries_ref[...].astype(F32)
-    key_pad[:, :tokens, :] = new_keys_ref[...].astype(F32)
-    value_pad[:, :tokens, :] = new_values_ref[...].astype(F32)
-    keys[:, cache:, :] = key_pad[...].astype(BF16)
-    values[:, cache:, :] = value_pad[...].astype(BF16)
+    def by_window(table, pad):
+        line = lax.broadcasted_iota(jnp.int32, (windows * pad, held), 0)
+        place = lax.broadcasted_iota(jnp.int32, (windows * pad, held), 1)
+        chosen = (line % pad < tokens) & (place == line % pad * windows + line // pad)
+        return jnp.dot(
+            jnp.where(chosen, 1.0, 0.0).astype(BF16), table, preferred_element_type=F32
+        )
+
+    fresh_pad = slots - cache
+    query_pad[...] = by_window(queries_ref[...], token_pad).reshape(query_pad.shape)
+    fresh_shape = (windows, fresh_pad, kv_width)
+    keys[:, cache:, :] = by_window(new_keys_ref[...], fresh_pad).reshape(fresh_shape).astype(BF16)
+    values[:, cache:, :] = (
+        by_window(new_values_ref[...], fresh_pad).reshape(fresh_shape).astype(BF16)
+    )
     kv_heads = kv_width // HD
     share_heads = depth // kv_width
     query_rows = share_heads * token_pad
     spot = lax.broadcasted_iota(jnp.int32, (query_rows, slots), 1)
     token = lax.broadcasted_iota(jnp.int32, (query_rows, slots), 0) % token_pad
     fresh_live = (spot >= cache) & (spot - cache <= token)
-    spot_float = spot.astype(F32)
 
     def attend(chosen_windows):
         units = [(w, k) for w in chosen_windows for k in range(kv_heads)]
@@ -148,7 +152,7 @@
             )
         weights = []
         for (w, _), score in zip(units, scores):
-            cached = (spot < cache) & (spot_float < lengths_ref[w : w + 1, 0:1])
+            cached = (spot < cache) & (spot < lengths_ref[w : w + 1, 0:1])
             score = jnp.where(cached | fresh_live, score, -1e30)
             powered = jnp.exp(score - jnp.max(score, axis=-1, keepdims=True))
             weights.append(
@@ -190,17 +194,14 @@
     attend(range(windows // 2, windows))
     attended = mixed[...].astype(BF16)
 
-    def pick(counts, count, table, tokens):
-        place = lax.broadcasted_iota(jnp.int32, (count, table.shape[0]), 1).astype(F32)
-        window = lax.broadcasted_iota(jnp.int32, (count, table.shape[0]), 0).astype(F32)
-        chosen = place == window * tokens + (counts - 1.0)
-        return jnp.dot(
-            jnp.where(chosen, 1.0, 0.0).astype(BF16), table, preferred_element_type=F32
-        )
-
     accepted_local.wait()
     near = accepted_near[pl.ds(pl.multiple_of(minor * windows, windows), windows), 0:1]
-    picked = pick(near, windows, attended, token_pad)
+    window = lax.broadcasted_iota(jnp.int32, (windows, windows * token_pad), 0)
+    place = lax.broadcasted_iota(jnp.int32, (windows, windows * token_pad), 1)
+    chosen = place == window * token_pad + near - 1
+    picked = jnp.dot(
+        jnp.where(chosen, 1.0, 0.0).astype(BF16), attended, preferred_element_type=F32
+    )
     first[pl.ds(pl.multiple_of(me_d * 2 * windows, 2 * windows), 2 * windows), :] = (
         jnp.concatenate([picked[:, :half], picked[:, half:]], axis=0).astype(BF16)
     )
@@ -320,7 +321,7 @@
         first_group(i).start()
     place = lax.broadcasted_iota(jnp.int32, (held, windows * token_pad), 1)
     row = lax.broadcasted_iota(jnp.int32, (held, windows * token_pad), 0)
-    compact = place == row // tokens * token_pad + row % tokens
+    compact = place == row % windows * token_pad + row // windows
     rows_all[pl.ds(pl.multiple_of(me_d * held, held), held), :] = jnp.dot(
         jnp.where(compact, 1.0, 0.0).astype(BF16), attended, preferred_element_type=F32
     ).astype(BF16)
@@ -333,7 +334,13 @@
             first_member(i, j).start()
     for i in turns[0]:
         all_group(i).start()
-    residual_picked = pick(accepted_ref[:, 0:1], rows, residual_ref[...], tokens)
+    residual_picked = jnp.zeros((rows, cols), F32)
+    for t in range(tokens):
+        residual_picked = jnp.where(
+            accepted_ref[:, 0:1] == t + 1,
+            residual_ref[t * rows : (t + 1) * rows, :].astype(F32),
+            residual_picked,
+        )
     load_out.wait()
     for i in order:
         for j in range(1, minors):
@@ -396,10 +403,15 @@
             slot = rows_in.at[source]
             pltpu.make_async_copy(slot, slot, rows_recv.at[source]).wait()
         for c in range(0, cols, 256):
-            total = rows_own[:, c : c + 256] + residual_ref[:, c : c + 256].astype(F32)
+            total = rows_own[:, c : c + 256]
             for k in range(1, nt):
                 total = total + rows_in[(me_t + k) % nt, :, c : c + 256].astype(F32)
-            verified_ref[:, c : c + 256] = total.astype(BF16)
+            total = total.reshape(minors, tokens, windows, 256)
+            for t in range(tokens):
+                spot = pl.ds(t * rows, rows)
+                verified_ref[spot, c : c + 256] = (
+                    total[:, t].reshape(rows, 256) + residual_ref[spot, c : c + 256].astype(F32)
+                ).astype(BF16)
 
     def early(s):
         for turn in range(spans + 1):
@@ -507,11 +519,11 @@
 
 
 def decode(nt, nd, queries, new_keys, new_values, lengths, accepted, residual, *large):
-    windows, tokens, depth = queries.shape
-    held = windows * tokens
+    held, depth = queries.shape
     span, cols = residual.shape
     rows = accepted.shape[0]
-    cache, kv_width = large[0].shape[1:]
+    windows, cache, kv_width = large[0].shape
+    tokens = held // windows
     token_pad = -(-tokens // 8) * 8
     fresh_pad = -(-tokens // 16) * 16
     minors = nd // nt
@@ -533,10 +545,8 @@
             pltpu.VMEM((windows, cache + fresh_pad, kv_width), BF16),
             pltpu.VMEM((windows, cache + fresh_pad, kv_width), BF16),
             pltpu.VMEM((windows, token_pad, depth), F32),
-            pltpu.VMEM((windows, fresh_pad, kv_width), F32),
-            pltpu.VMEM((windows, fresh_pad, kv_width), F32),
             pltpu.VMEM((windows * token_pad, depth), F32),
-            pltpu.VMEM(accepted.shape, F32),
+            pltpu.VMEM(accepted.shape, jnp.int32),
             pltpu.VMEM((nd * 2 * windows, depth // 2), BF16),
             pltpu.VMEM((STEPS + 1, CUTS, rows, part), BF16),
             pltpu.VMEM((STEPS, CUTS, nt - 1, rows, part), BF16),
@@ -567,7 +577,7 @@
             dma((nt,)),
         ],
         compiler_params=pltpu.CompilerParams(
-            collective_id=0, has_side_effects=True, vmem_limit_bytes=48 * 1024 * 1024
+            collective_id=0, has_side_effects=True, vmem_limit_bytes=62 * 1024 * 1024
         ),
         cost_estimate=pl.CostEstimate(
             flops=2 * (STEPS * nt * rows + nd * held) * depth * cols,
@@ -589,22 +599,26 @@
     out_weight,
     draft_weight,
 ):
+    def flat(table):
+        return jnp.swapaxes(table, 0, 1).reshape(-1, table.shape[2])
+
     block_windows, block_tokens, block_cols = residual.shape
     verified, drafted = decode(
         lax.axis_size("tensor"),
         lax.axis_size("dp"),
-        queries,
-        new_keys,
-        new_values,
-        jnp.broadcast_to(cache_lengths.astype(F32)[:, None], (cache_lengths.shape[0], HD)),
-        jnp.broadcast_to(accepted.astype(F32)[:, None], (block_windows, HD)),
-        residual.reshape(block_windows * block_tokens, block_cols),
+        flat(queries),
+        flat(new_keys),
+        flat(new_values),
+        jnp.broadcast_to(cache_lengths[:, None], (cache_lengths.shape[0], HD)),
+        jnp.broadcast_to(accepted[:, None], (block_windows, HD)),
+        flat(residual),
         key_cache,
         value_cache,
         out_weight,
         draft_weight,
     )
-    return (verified.reshape(residual.shape), drafted)
+    verified = verified.reshape(block_tokens, block_windows, block_cols)
+    return (jnp.swapaxes(verified, 0, 1), drafted)
 
 
 def solution(mesh):

time: 100 us -> 98.8 us (0.988)
  Pallas kernels: 90 us -> 92.1 us
  local copies, waits for them, and re-layouts: 7.76 us -> 5.85 us
  other arithmetic: 1.32 us -> 0 us
    unnamed x10 -> x2, local copies, waits for them, and re-layouts: 7.48 us -> 3.21 us
    broadcast_in_dim x2, local copies, waits for them, and re-layouts: 0.14 us -> 2.64 us  [the longest x1 1.32 us: per_device(): jnp.broadcast_to(accepted[:, None], (block_windows, HD))]
    pallas_call x1, Pallas kernels: 90 us -> 92.1 us  [decode(): pl.pallas_call(functools.partial(decode_kernel, nt, nd), out_shape=(jax.S...]
    convert_element_type x2 -> x0, other arithmetic: 1.32 us -> none  [the longest x1 0.66 us: per_device(): cache_lengths.astype(F32)[:, None]]
where the time goes in v5:
time: 98.8 us; the launch traced here: 98.6 us
  Pallas kernels  92.1 us (93%)
  local copies, waits for them, and re-layouts  5.85 us (6%)
    pallas_call x1, Pallas kernels, decode(): pl.pallas_call(functools.partial(decode_kernel, nt, nd), out_shape=(jax.S...  92.1 us
    unnamed x2, local copies, waits for them, and re-layouts  3.21 us

profile of v5, /device:TPU:0, one launch (start us, length us, event | category | flops | bytes accessed | tf_op | source)
XLA Modules:
  0.0 98.6 jit_solution(6452217425086620597)
XLA Ops:
  0.6 1.3 %broadcast_in_dim.4.lengths_ref = s32[8,128]{1,0:T(8,128)} broadcast(s32[8]{0:T(128)} %param.15), dimensions={0} | broadcast | bytes 4128 | tf_op jit(solution)/shard_map/broadcast_in_dim | solution.py:612
  1.9 1.3 %broadcast_in_dim.5.accepted_ref = s32[16,128]{1,0:T(8,128)} broadcast(s32[16]{0:T(128)} %param.16), dimensions={0} | broadcast | bytes 8256 | tf_op jit(solution)/shard_map/broadcast_in_dim | solution.py:613
  3.3 92.1 %shard_map.113 = (bf16[96,1024]{1,0:T(8,128)(2,1)}, bf16[5,16,1024]{2,1,0:T(8,128)(2,1)}) custom-call(bf16[48,2048]{1,0:T(8,128)(2,1)} %bitcast.16, bf16[48,256]{1,0:T(8,128)(2,1)} %bitcast.18, bf16[48,256]{1,0:T(8,128)(2,1)} %bitcast.19, s32[8,128]{1,0:T(8,128)} %broadcast_in_dim.4.lengths_ref, s32[16,128]{1,0:T(8,128)} %broadcast_in_dim.5.accepted_ref, ...), custom_call_target="tpu_custom_call" | custom-call | flops 2952790016 | bytes 8388608 | tf_op jit(solution)/shard_map/pallas_call | solution.py:534
  95.3 1.6 %copy.14 = bf16[16,6,1024]{2,0,1:T(8,128)(2,1)} copy(bf16[16,6,1024]{2,0,1:T(8,128)(2,1)} %bitcast.15) | data formatting | bytes 393216
  97.0 1.6 %copy.15 = bf16[5,16,1024]{2,1,0:T(8,128)(2,1)} copy(bf16[5,16,1024]{2,1,0:T(8,128)(2,1)} %get-tuple-element.9) | data formatting | bytes 327680

commit v6 on v5

--- a/solution.py
+++ b/solution.py
@@ -374,23 +374,28 @@
             device_id_type=MESH,
         )
 
-    def project(i):
-        for j in range(1, minors):
-            all_arrived(i, j)
+    def project(i, n):
+        if n == 0:
+            for j in range(1, minors):
+                all_arrived(i, j)
         target = (group + nt - i) % nt
         span = minors * held
         block = rows_all.at[pl.ds(pl.multiple_of(target * span, span), span)]
-        for c in range(0, cols, 256):
-            product = jnp.dot(block[...], out_weight[:, c : c + 256], preferred_element_type=F32)
-            rows_out[i, :, c : c + 256] = product.astype(BF16)
+        for c in range(n * part, (n + 1) * part, chunk):
+            product = jnp.dot(
+                block[...], out_weight[:, c : c + chunk], preferred_element_type=F32
+            )
+            rows_out[i, :, c : c + chunk] = product.astype(BF16)
 
             @pl.when(target == me_t)
             def _():
-                rows_own[:, c : c + 256] = product
-
-        @pl.when(target != me_t)
-        def _():
-            rows_copy(i).start()
+                rows_own[:, c : c + chunk] = product
+
+        if n == CUTS - 1:
+
+            @pl.when(target != me_t)
+            def _():
+                rows_copy(i).start()
 
     def forward(i):
         all_arrived(i, 0)
@@ -421,19 +426,22 @@
                 for i in turns[turn] if turn < spans else []:
                     forward(i)
                 for i in turns[turn - 1] if turn else order[:1]:
-                    project(i)
+                    project(i, 0)
 
         @pl.when(s == spans + 1)
         def _():
             collect()
 
     def late(s):
-        for turn in range(1, spans):
-
-            @pl.when(s == turn - 1)
+        for turn in range(spans + 1):
+
+            @pl.when(s == turn)
             def _(turn=turn):
-                for i in turns[turn]:
+                for i in turns[turn + 1] if turn + 1 < spans else []:
                     all_group(i).start()
+                for i in turns[turn - 1] if turn else order[:1]:
+                    for n in range(1, CUTS):
+                        project(i, n)
 
     def step(s, carry):
         early(s)
@@ -577,7 +585,7 @@
             dma((nt,)),
         ],
         compiler_params=pltpu.CompilerParams(
-            collective_id=0, has_side_effects=True, vmem_limit_bytes=62 * 1024 * 1024
+            collective_id=0, has_side_effects=True, vmem_limit_bytes=48 * 1024 * 1024
         ),
         cost_estimate=pl.CostEstimate(
             flops=2 * (STEPS * nt * rows + nd * held) * depth * cols,

time: 98.8 us -> 95.8 us (0.970)
  Pallas kernels: 92.1 us -> 86.2 us
  local copies, waits for them, and re-layouts: 5.85 us -> 8.57 us
    pallas_call x1, Pallas kernels: 92.1 us -> 86.2 us  [decode(): pl.pallas_call(functools.partial(decode_kernel, nt, nd), out_shape=(jax.S...]
    unnamed x2 -> x14, local copies, waits for them, and re-layouts: 3.21 us -> 7.12 us
where the time goes in v6:
time: 95.8 us; the launch traced here: 95.4 us
  Pallas kernels  86.2 us (90%)
  local copies, waits for them, and re-layouts  8.57 us (9%)
    pallas_call x1, Pallas kernels, decode(): pl.pallas_call(functools.partial(decode_kernel, nt, nd), out_shape=(jax.S...  86.2 us
    unnamed x14, local copies, waits for them, and re-layouts  7.12 us

profile of v6, /device:TPU:0, one launch (start us, length us, event | category | flops | bytes accessed | tf_op | source)
XLA Modules:
  0.0 95.4 jit_solution(10141325719373444290)
XLA Ops:
  0.6 0.7 broadcast_in_dim.4.lengths_ref
  1.4 0.7 broadcast_in_dim.5.accepted_ref
  2.1 0.0 copy-start
  2.1 1.2 %copy-done = bf16[8,256,256]{2,1,0:T(8,128)(2,1)S(1)} copy-done((bf16[8,256,256]{2,1,0:T(8,128)(2,1)S(1)}, bf16[8,256,256]{2,1,0:T(8,128)(2,1)}, u32[]{:S(2)}) %copy-start) | copy-done | bytes 1048600
  3.3 0.0 copy-start.1
  3.3 1.2 %copy-done.1 = bf16[8,256,256]{2,1,0:T(8,128)(2,1)S(1)} copy-done((bf16[8,256,256]{2,1,0:T(8,128)(2,1)S(1)}, bf16[8,256,256]{2,1,0:T(8,128)(2,1)}, u32[]{:S(2)}) %copy-start.1) | copy-done | bytes 1048600
  4.5 0.0 copy-start.2
  4.5 0.9 copy-done.2
  5.5 0.0 copy-start.3
  5.5 0.9 copy-done.3
  6.4 0.0 copy-start.4
  6.4 0.7 copy-done.4
  7.1 0.0 copy-start.5
  7.1 0.7 copy-done.5
  7.9 86.2 %shard_map.113 = (bf16[96,1024]{1,0:T(8,128)(2,1)S(1)}, bf16[5,16,1024]{2,1,0:T(8,128)(2,1)S(1)}) custom-call(bf16[48,2048]{1,0:T(8,128)(2,1)S(1)} %bitcast.16, bf16[48,256]{1,0:T(8,128)(2,1)S(1)} %bitcast.18, bf16[48,256]{1,0:T(8,128)(2,1)S(1)} %bitcast.19, s32[8,128]{1,0:T(8,128)S(1)} %broadcast_in_dim.4.lengths_ref, ...), custom_call_target="tpu_custom_call" | custom-call | flops 2952790016 | bytes 8388608 | tf_op jit(solution)/shard_map/pallas_call | solution.py:542
  94.0 0.7 copy.14
  94.7 0.7 copy.15
Async XLA Ops:
  2.1 1.2 %copy-start = (bf16[8,256,256]{2,1,0:T(8,128)(2,1)S(1)}, bf16[8,256,256]{2,1,0:T(8,128)(2,1)}, u32[]{:S(2)}) copy-start(bf16[8,256,256]{2,1,0:T(8,128)(2,1)} %key_cache_hbm.1) | copy-start | bytes 3145732
  3.3 1.2 %copy-start.1 = (bf16[8,256,256]{2,1,0:T(8,128)(2,1)S(1)}, bf16[8,256,256]{2,1,0:T(8,128)(2,1)}, u32[]{:S(2)}) copy-start(bf16[8,256,256]{2,1,0:T(8,128)(2,1)} %value_cache_hbm.1) | copy-start | bytes 3145732
  4.5 0.9 copy-start.2
  5.5 0.9 copy-start.3
  6.4 0.7 copy-start.4
  7.1 0.7 copy-start.5

commit v7 on v6

--- a/solution.py
+++ b/solution.py
@@ -585,7 +585,7 @@
             dma((nt,)),
         ],
         compiler_params=pltpu.CompilerParams(
-            collective_id=0, has_side_effects=True, vmem_limit_bytes=48 * 1024 * 1024
+            collective_id=0, has_side_effects=True, vmem_limit_bytes=62 * 1024 * 1024
         ),
         cost_estimate=pl.CostEstimate(
             flops=2 * (STEPS * nt * rows + nd * held) * depth * cols,

time: 95.8 us -> 96.3 us (level)
  Pallas kernels: 86.2 us -> 89.6 us
  local copies, waits for them, and re-layouts: 8.57 us -> 5.85 us
    unnamed x14 -> x2, local copies, waits for them, and re-layouts: 7.12 us -> 3.21 us
    pallas_call x1, Pallas kernels: 86.2 us -> 89.6 us  [decode(): pl.pallas_call(functools.partial(decode_kernel, nt, nd), out_shape=(jax.S...]
where the time goes in v7:
time: 96.3 us; the launch traced here: 96 us
  Pallas kernels  89.6 us (93%)
  local copies, waits for them, and re-layouts  5.85 us (6%)
    pallas_call x1, Pallas kernels, decode(): pl.pallas_call(functools.partial(decode_kernel, nt, nd), out_shape=(jax.S...  89.6 us
    unnamed x2, local copies, waits for them, and re-layouts  3.21 us

profile of v7, /device:TPU:0, one launch (start us, length us, event | category | flops | bytes accessed | tf_op | source)
XLA Modules:
  0.0 96.0 jit_solution(13932308009796611422)
XLA Ops:
  0.6 1.3 %broadcast_in_dim.4.lengths_ref = s32[8,128]{1,0:T(8,128)} broadcast(s32[8]{0:T(128)} %param.15), dimensions={0} | broadcast | bytes 4128 | tf_op jit(solution)/shard_map/broadcast_in_dim | solution.py:620
  1.9 1.3 %broadcast_in_dim.5.accepted_ref = s32[16,128]{1,0:T(8,128)} broadcast(s32[16]{0:T(128)} %param.16), dimensions={0} | broadcast | bytes 8256 | tf_op jit(solution)/shard_map/broadcast_in_dim | solution.py:621
  3.3 89.6 %shard_map.113 = (bf16[96,1024]{1,0:T(8,128)(2,1)}, bf16[5,16,1024]{2,1,0:T(8,128)(2,1)}) custom-call(bf16[48,2048]{1,0:T(8,128)(2,1)} %bitcast.16, bf16[48,256]{1,0:T(8,128)(2,1)} %bitcast.18, bf16[48,256]{1,0:T(8,128)(2,1)} %bitcast.19, s32[8,128]{1,0:T(8,128)} %broadcast_in_dim.4.lengths_ref, s32[16,128]{1,0:T(8,128)} %broadcast_in_dim.5.accepted_ref, ...), custom_call_target="tpu_custom_call" | custom-call | flops 2952790016 | bytes 8388608 | tf_op jit(solution)/shard_map/pallas_call | solution.py:542
  92.8 1.6 %copy.14 = bf16[16,6,1024]{2,0,1:T(8,128)(2,1)} copy(bf16[16,6,1024]{2,0,1:T(8,128)(2,1)} %bitcast.15) | data formatting | bytes 393216
  94.5 1.6 %copy.15 = bf16[5,16,1024]{2,1,0:T(8,128)(2,1)} copy(bf16[5,16,1024]{2,1,0:T(8,128)(2,1)} %get-tuple-element.9) | data formatting | bytes 327680
